TPU v7x, 512 devices: a whole 4x4x16 slice. The times are simulated.
512 devices in a mesh: var: 16 (over z), lat: 32 (over x, y, core).
Axes of the slice: x: 4, y: 4, z: 16, core: 2. Of those that a mesh axis runs over, the one named last changes fastest.
Arguments:
- fields: bfloat16 [32, 16, 16384], P('var', None, 'lat'), may hold values from -6 to 6
- owner_table: int32 [16], replicated, may hold values from 0 to 15, as said below
- band_tokens: int32 [32], replicated, may hold values from 1 to 512, 12288 in all
- patch_weight: bfloat16 [32, 16, 1024], P('var'), may hold values from -1.5 to 1.5
- var_embed: bfloat16 [16, 1024], replicated, may hold values from -6 to 6
- key_query: bfloat16 [1024, 16], replicated, may hold values from -0.1875 to 0.1875
- value_weight: bfloat16 [1024, 1024], replicated, may hold values from -0.1875 to 0.1875
- out_weight: bfloat16 [1024, 1024], replicated, may hold values from -0.1875 to 0.1875
- cotangent: bfloat16 [32, 512, 1024], P('lat', 'var'), may hold values from -0.5 to 0.5
Outputs:
- aggregated: bfloat16 [32, 512, 1024], P('lat', 'var')
- d_value_weight: float32 [1024, 1024], P('lat')
- d_patch_weight: float32 [32, 16, 1024], P('var')
Inputs may be any that keep to these rules, and one draw needn't show every extreme that they name: `owner_table`: each index of var owns at most 2 variables, and one owns exactly 2. The valid tokens of a band are its first band_tokens of 512; some band is full.
All inputs are finite; a program needn't handle non-finite values.
Results may differ from a plain program's by a relative error of at most 0.03.
Values may be sent and summed in bfloat16 or wider, within the bound.
A program may use at most 64 MiB of HBM per device.

v0:
```python
import jax
import jax.numpy as jnp
from jax import lax
from jax.sharding import PartitionSpec as P


def slot_table(owner_table, slot_count):
    var_ids = jnp.arange(owner_table.shape[0], dtype=jnp.int32)
    same_owner = owner_table[:, None] == owner_table[None, :]
    earlier_var = var_ids[None, :] < var_ids[:, None]
    var_rank = jnp.sum((same_owner & earlier_var).astype(jnp.int32), axis=1)
    return owner_table * slot_count + var_rank


def per_device(
    fields,
    owner_table,
    band_tokens,
    patch_weight,
    var_embed,
    key_query,
    value_weight,
    out_weight,
    cotangent,
):
    var_count = lax.axis_size("var")
    slot_count = fields.shape[0]
    slot_total = slot_count * var_count
    tok_lat = fields.shape[2]
    tok_dev = tok_lat // var_count
    model_width = value_weight.shape[0]
    head_count = key_query.shape[1]
    head_dim = model_width // head_count
    variables = owner_table.shape[0]
    var_index = lax.axis_index("var")
    lat_index = lax.axis_index("lat")
    var_slot = slot_table(owner_table, slot_count)
    slot_match = (jnp.arange(slot_total, dtype=jnp.int32)[:, None] == var_slot[None, :]).astype(
        jnp.float32
    )
    local_match = lax.dynamic_slice_in_dim(slot_match, var_index * slot_count, slot_count, 0)
    band_count = jnp.sum(
        jnp.where(jnp.arange(band_tokens.shape[0], dtype=jnp.int32) == lat_index, band_tokens, 0)
    )
    token_rows = var_index * tok_dev + jnp.arange(tok_dev, dtype=jnp.int32)
    valid_mask = (token_rows < band_count).astype(jnp.float32)[:, None]
    embed_bias = jnp.dot(
        local_match, var_embed.astype(jnp.float32), precision=lax.Precision.HIGHEST
    )
    local_tokens = jnp.einsum(
        "skt,skd->std", fields, patch_weight, preferred_element_type=jnp.float32
    )
    local_tokens = (local_tokens + embed_bias[:, None, :]).astype(jnp.bfloat16)
    received = lax.all_to_all(local_tokens, "var", split_axis=1, concat_axis=0, tiled=True)
    embedded = received[var_slot]
    flattened = embedded.reshape(variables * tok_dev, model_width)
    scores = jnp.dot(flattened, key_query, preferred_element_type=jnp.float32).reshape(
        variables, tok_dev, head_count
    )
    exponent = jnp.exp(scores)
    attention = exponent / jnp.sum(exponent, axis=0)
    values = jnp.dot(flattened, value_weight, preferred_element_type=jnp.float32).astype(
        jnp.bfloat16
    )
    values = values.reshape(variables, tok_dev, head_count, head_dim).astype(jnp.float32)
    pooled = (
        jnp.sum(attention[..., None] * values, axis=0)
        .astype(jnp.bfloat16)
        .reshape(tok_dev, model_width)
    )
    aggregated = (
        valid_mask * jnp.dot(pooled, out_weight, preferred_element_type=jnp.float32)
    ).astype(jnp.bfloat16)
    masked = valid_mask.astype(jnp.bfloat16) * cotangent[0]
    head_grads = jnp.dot(masked, out_weight.T, preferred_element_type=jnp.float32).astype(
        jnp.bfloat16
    )
    head_grads = head_grads.reshape(tok_dev, head_count, head_dim).astype(jnp.float32)
    dvalues = (
        (attention[..., None] * head_grads[None])
        .astype(jnp.bfloat16)
        .reshape(variables * tok_dev, model_width)
    )
    dweights = jnp.sum(head_grads[None] * values, axis=-1)
    dscores = attention * (dweights - jnp.sum(attention * dweights, axis=0))
    shard_rows = lax.psum_scatter(
        lax.dot_general(
            flattened, dvalues, (((0,), (0,)), ((), ())), preferred_element_type=jnp.float32
        ).astype(jnp.bfloat16),
        "lat",
        scatter_dimension=0,
        tiled=True,
    )
    d_value_weight = lax.psum(shard_rows, "var").astype(jnp.float32)
    embed_grad = jnp.dot(dvalues, value_weight.T, preferred_element_type=jnp.float32)
    embed_grad = embed_grad + jnp.dot(
        dscores.reshape(variables * tok_dev, head_count),
        key_query.astype(jnp.float32).T,
        precision=lax.Precision.HIGHEST,
    )
    embed_grad = embed_grad.astype(jnp.bfloat16).reshape(variables, tok_dev, model_width)
    slot_grads = (
        jnp.zeros((slot_total, tok_dev, model_width), jnp.bfloat16).at[var_slot].set(embed_grad)
    )
    returned = lax.all_to_all(slot_grads, "var", split_axis=0, concat_axis=1, tiled=True)
    partial_grads = jnp.einsum("skt,std->skd", fields, returned, preferred_element_type=jnp.float32)
    d_patch_weight = lax.psum(partial_grads.astype(jnp.bfloat16), "lat").astype(jnp.float32)
    return (aggregated[None], d_value_weight, d_patch_weight)


def solution(mesh):
    in_specs = (
        P("var", None, "lat"),
        P(),
        P(),
        P("var", None, None),
        P(),
        P(),
        P(),
        P(),
        P("lat", "var", None),
    )
    out_specs = (P("lat", "var", None), P("lat", None), P("var", None, None))
    return jax.shard_map(
        per_device, mesh=mesh, in_specs=in_specs, out_specs=out_specs, check_vma=False
    )
```

profile of v0, /device:TPU:1, one launch (start us, length us, event | category | flops | bytes accessed | tf_op | source)
XLA Modules:
  0.0 550.1 jit_solution(4310058925865889982)
XLA Ops:
  9.7 1.6 add_convert_fusion
  11.3 3.5 copy.31
  14.8 15.9 %all-to-all-start = ((bf16[2,512,1024]{2,0,1:T(2,128)(2,1)}), bf16[2,512,1024]{2,0,1:T(2,128)(2,1)}, u32[]{:S(2)}, u32[]{:S(2)}) async-start(bf16[2,512,1024]{2,0,1:T(2,128)(2,1)} %copy.31), calls=%async_computation | async-start | bytes 4194304 | tf_op jit(solution)/shard_map/all_to_all | solution.py:54
  32.1 2.3 fusion.2
  34.5 88.1 %all-to-all-done = bf16[2,512,1024]{2,0,1:T(2,128)(2,1)} async-done(((bf16[2,512,1024]{2,0,1:T(2,128)(2,1)}), bf16[2,512,1024]{2,0,1:T(2,128)(2,1)}, u32[]{:S(2)}, u32[]{:S(2)}) %all-to-all-start) | async-done | bytes 2097184 | tf_op jit(solution)/shard_map/all_to_all | solution.py:54
  122.6 2.2 copy.32
  126.4 2.2 gather_fusion
  128.6 1.6 fusion.16
  130.8 1.7 copy.34
  132.6 2.6 fusion
  135.2 4.5 reshape.67
  139.7 5.7 %multiply_reduce_fusion = (f32[16,32,16]{2,1,0:T(8,128)}, bf16[32,16,64]{2,1,0:T(8,128)(2,1)}, bf16[16,32,16,64]{3,2,1,0:T(8,128)(2,1)}) fusion(f32[16,32,16,64]{3,2,1,0:T(8,128)} %reshape.67, f32[32,16,64]{2,1,0:T(8,128)S(1)} %reshape.68, f32[16,32,16]{2,1,0:T(8,128)} %copy.34), kind=kLoop, calls=%fused_computation.2 | loop fusion | flops 3104768 | bytes 3407872 | tf_op jit(solution)/shard_map/reduce_sum | solution.py:84
  146.7 4.1 convert_element_type.105
  150.8 2.5 fusion.17
  153.3 2.1 add_convert_fusion.1
  155.4 1.6 broadcast_in_dim.13
  157.0 3.5 scatter_fusion
  160.5 11.2 %all-to-all-start.1 = ((bf16[32,32,1024]{2,1,0:T(8,128)(2,1)}), bf16[32,32,1024]{2,1,0:T(8,128)(2,1)}, u32[]{:S(2)}, u32[]{:S(2)}) async-start(bf16[32,32,1024]{2,1,0:T(8,128)(2,1)} %scatter_fusion), calls=%async_computation.2 | async-start | bytes 4194304 | tf_op jit(solution)/shard_map/all_to_all | solution.py:105
  171.8 3.8 convolution_convert_fusion
  176.6 102.0 %reduce-scatter.2.cloned.1.call-done = bf16[32,1024]{1,0:T(8,128)(2,1)} async-done(((bf16[1024,1024]{1,0:T(8,128)(2,1)}), bf16[32,1024]{1,0:T(8,128)(2,1)}) %reduce-scatter.2.cloned.1.call-update) | async-done | bytes 65552 | tf_op jit(solution)/shard_map/reduce_scatter | solution.py:86
  278.7 1.8 copy.38
  281.6 2.7 fusion.4
  284.2 120.2 %all-reduce.3.cloned.1.call-done = bf16[32,1024]{1,0:T(8,128)(2,1)} async-done(((bf16[32,1024]{1,0:T(8,128)(2,1)}), bf16[32,1024]{1,0:T(8,128)(2,1)}) %all-reduce.3.cloned.1.call-update) | async-done | bytes 65552 | tf_op jit(solution)/shard_map/psum | solution.py:94
  405.9 136.1 %all-reduce.5.cloned.1.call-done = bf16[2,16,1024]{2,1,0:T(8,128)(2,1)} async-done(((bf16[2,16,1024]{2,1,0:T(8,128)(2,1)}), bf16[2,16,1024]{2,1,0:T(8,128)(2,1)}) %all-reduce.5.cloned.1.call-update) | async-done | bytes 65552 | tf_op jit(solution)/shard_map/psum | solution.py:107
  (37 shorter events, 12.6 us)
Async XLA Ops:
  7.2 125.4 %copy-start = (bf16[1024,1024]{1,0:T(8,128)(2,1)S(1)}, bf16[1024,1024]{1,0:T(8,128)(2,1)}, u32[]{:S(2)}) copy-start(bf16[1024,1024]{1,0:T(8,128)(2,1)} %param.15) | copy-start | bytes 6291460
  14.8 16.0 %copy-start.5 = (s32[32]{0:T(128)S(1)}, s32[32]{0:T(128)}, u32[]{:S(2)}) copy-start(s32[32]{0:T(128)} %param.11) | copy-start | bytes 388
  14.8 17.2 %copy-start.4 = (bf16[1,32,1024]{2,1,0:T(8,128)(2,1)S(1)}, bf16[1,32,1024]{2,1,0:T(8,128)(2,1)}, u32[]{:S(2)}) copy-start(bf16[1,32,1024]{2,1,0:T(8,128)(2,1)} %param.17) | copy-start | bytes 196612
  14.8 107.8 %all-to-all-start = ((bf16[2,512,1024]{2,0,1:T(2,128)(2,1)}), bf16[2,512,1024]{2,0,1:T(2,128)(2,1)}, u32[]{:S(2)}, u32[]{:S(2)}) async-start(bf16[2,512,1024]{2,0,1:T(2,128)(2,1)} %copy.31), calls=%async_computation | async-start | bytes 4194304 | tf_op jit(solution)/shard_map/all_to_all | solution.py:54
  150.8 2.5 copy-start.3
  160.5 118.2 %all-to-all-start.1 = ((bf16[32,32,1024]{2,1,0:T(8,128)(2,1)}), bf16[32,32,1024]{2,1,0:T(8,128)(2,1)}, u32[]{:S(2)}, u32[]{:S(2)}) async-start(bf16[32,32,1024]{2,1,0:T(8,128)(2,1)} %scatter_fusion), calls=%async_computation.2 | async-start | bytes 4194304 | tf_op jit(solution)/shard_map/all_to_all | solution.py:105
  171.7 106.9 %reduce-scatter.2.cloned.1.call-start = ((), (), s32[]{:S(2)}) async-start(), calls=%async_computation.3 | async-start | bytes 2162688 | tf_op jit(solution)/shard_map/reduce_scatter | solution.py:86
  175.6 0.9 copy-start.1
  175.6 228.8 %all-reduce.3.cloned.1.call-start = ((), (), s32[]{:S(2)}) async-start(), calls=%async_computation.4 | async-start | bytes 131072 | tf_op jit(solution)/shard_map/psum | solution.py:94
  278.7 263.4 %all-reduce.5.cloned.1.call-start = ((), (), s32[]{:S(2)}) async-start(), calls=%async_computation.5 | async-start | bytes 131072 | tf_op jit(solution)/shard_map/psum | solution.py:107
  278.7 1.8 copy-start.2
Sparse Core Ops, SparseCore 0:
  177.0 101.6 reduce-scatter.1
  281.0 123.4 all-reduce.2
  408.6 133.3 all-reduce.4
where the time goes:
time: 551 us; the launch traced here: 550 us
  waiting for transfers between devices  447 us (81%)
  local copies, waits for them, and re-layouts  28.9 us (5%)
  starting transfers between devices  27.3 us (5%)
  matrix products  21.1 us (4%)
  between operations  13.9 us (3%)
  other arithmetic  12.4 us (2%)
    psum x1, waiting for transfers between devices, per_device(): lax.psum(partial_grads.astype(jnp.bfloat16), 'lat').astype(jnp.float32)  136 us
    psum x1, waiting for transfers between devices, per_device(): d_value_weight = lax.psum(shard_rows, 'var').astype(jnp.float32)  120 us
    reduce_scatter x1, waiting for transfers between devices, per_device(): lax.psum_scatter(lax.dot_general(flattened, dvalues, (((0,), (0,)), ((),...  102 us
    all_to_all x1, waiting for transfers between devices, per_device(): lax.all_to_all(local_tokens, 'var', split_axis=1, concat_axis=0, tiled=True)  88.1 us
    all_to_all x1, starting transfers between devices, per_device(): lax.all_to_all(local_tokens, 'var', split_axis=1, concat_axis=0, tiled=True)  15.9 us
    all_to_all x1, starting transfers between devices, per_device(): lax.all_to_all(slot_grads, 'var', split_axis=0, concat_axis=1, tiled=True)  11.2 us
  transfers between devices with their start and end apart: 5, of which 4 were waited for; matrix products, arithmetic and copies ran while one was open for 3% of the time, Pallas kernels for 0%

commit v1 on v0

v1 whole, which is shorter than its diff:
```python
import functools

import jax
import jax.numpy as jnp
from jax import lax
from jax.experimental import pallas as pl
from jax.experimental.pallas import tpu as pltpu
from jax.sharding import PartitionSpec as P

MESH = pl.DeviceIdType.MESH
F32 = jnp.float32
BF16 = jnp.bfloat16

NZ = 16
NP = 16
V = 16
K = 16
T = 32
D = 1024
TILES = 9
VK = V * K
TOK = NP * T


def dot(a, b, ca=1, cb=0):
    return lax.dot_general(a, b, (((ca,), (cb,)), ((), ())), preferred_element_type=F32)


def pooling_kernel(
    owner_ref,
    band_ref,
    fields_hbm,
    pw_hbm,
    ve_hbm,
    kq_hbm,
    vw_hbm,
    ow_hbm,
    cot_hbm,
    agg_ref,
    dvw_ref,
    dpw_ref,
    fields_v,
    pwve,
    kq_v,
    vwg,
    vw_v,
    ow_v,
    cot_v,
    msg1,
    recv1,
    krow,
    recvk,
    hmsg,
    recvh,
    mm,
    tmsg,
    recvf,
    recvp,
    aa,
    pmsg,
    recvpool,
    gtile,
    recvr,
    red,
    gtot,
    msg5,
    recv5,
    srow,
    recvs,
    load_sem,
    send_sem,
    recv_sem,
):
    z = lax.axis_index("var")
    lat = lax.axis_index("lat")
    core = lax.rem(lat, 2)
    p = lat // 2

    def zpeer(d):
        return {"var": lax.rem(z + d, NZ), "lat": lat}

    def plane_peer(chip):
        return {"var": z, "lat": chip * 2 + core}

    barrier = pltpu.get_barrier_semaphore()

    def signal_z(d, carry):
        pl.semaphore_signal(barrier, inc=1, device_id=zpeer(d), device_id_type=MESH)
        other = {"var": lax.rem(z + d, NZ), "lat": p * 2 + 1 - core}
        pl.semaphore_signal(barrier, inc=1, device_id=other, device_id_type=MESH)
        chip = lax.rem(p + d, NP)
        pl.semaphore_signal(barrier, inc=1, device_id=plane_peer(chip), device_id_type=MESH)
        return carry

    lax.fori_loop(1, NZ, signal_z, 0)
    pl.semaphore_signal(
        barrier, inc=1, device_id={"var": z, "lat": p * 2 + 1 - core}, device_id_type=MESH
    )

    group = pl.multiple_of((p // 2) * 128, 128)
    loads = [
        pltpu.make_async_copy(pw_hbm, pwve.at[pl.ds(0, 32)], load_sem.at[0]),
        pltpu.make_async_copy(ve_hbm, pwve.at[pl.ds(32, 16)], load_sem.at[1]),
        pltpu.make_async_copy(vw_hbm.at[:, pl.ds(group, 128)], vwg, load_sem.at[2]),
        pltpu.make_async_copy(kq_hbm, kq_v, load_sem.at[3]),
        pltpu.make_async_copy(fields_hbm, fields_v, load_sem.at[4]),
        pltpu.make_async_copy(cot_hbm, cot_v, load_sem.at[5]),
        pltpu.make_async_copy(ow_hbm, ow_v, load_sem.at[6]),
        pltpu.make_async_copy(vw_hbm, vw_v, load_sem.at[7]),
    ]
    for load in loads:
        load.start()

    owners = [owner_ref[v] for v in range(V)]
    slots = []
    for v in range(V):
        rank = jnp.int32(0)
        for u in range(v):
            rank = rank + (owners[u] == owners[v]).astype(jnp.int32)
        slots.append(owners[v] * 2 + rank)
    held = []
    for s in range(2):
        var_of, has = jnp.int32(0), jnp.int32(0)
        for v in range(V):
            hit = (slots[v] == 2 * z + s).astype(jnp.int32)
            var_of, has = var_of + hit * v, has + hit
        held.append((var_of, has))

    lane16 = lax.broadcasted_iota(jnp.int32, (16, 128), 1)
    row16 = lax.broadcasted_iota(jnp.int32, (16, 128), 0)
    lane32 = lax.broadcasted_iota(jnp.int32, (32, 128), 1)
    row32 = lax.broadcasted_iota(jnp.int32, (32, 128), 0)

    for i in range(5):
        loads[i].wait()
    turn = lax.rem(p, 2) * 64
    both = pwve[...]
    head_cols = pltpu.roll(dot(both, vwg[...]), turn, 1)
    key_cols = dot(both, kq_v[...])
    key_lane = lax.broadcasted_iota(jnp.int32, (48, 16), 1)
    key_col = jnp.sum(jnp.where(key_lane == p, key_cols, 0.0), axis=1, keepdims=True)
    key_bias = key_col[32:48]
    krow[...] = jnp.sum(
        jnp.where(lane32 == row32, key_col[0:32], 0.0), axis=0, keepdims=True
    )
    mm[V] = jnp.where(lane16 < 64, head_cols[32:48], 0.0).astype(BF16)
    slot_cols = head_cols[0:32]
    own_group = pl.multiple_of((lat // 4) * 128, 128)
    own_cols = pltpu.roll(
        pwve[pl.ds(0, 32), pl.ds(own_group, 128)].astype(F32),
        lax.rem(224 - 32 * lax.rem(lat, 4), 128),
        1,
    )
    base = jnp.where(lane32 < 64, slot_cols, own_cols)
    for q in range(4):
        tokens = fields_v[:, :, 128 * q : 128 * q + 128].reshape(32, 128).astype(F32)
        for r in range(4):
            turned = pltpu.roll(tokens, (64 - 32 * r) % 128, 1) if r != 2 else tokens
            piece = jnp.where((lane32 >= 64) & (lane32 < 96), turned, base)
            msg1[4 * q + r] = piece.astype(BF16).reshape(2, 16, 128)

    pl.semaphore_wait(barrier, 46)

    def copy1(d):
        return pltpu.make_async_remote_copy(
            src_ref=msg1.at[lax.rem(z + d, NZ)],
            dst_ref=recv1.at[pl.ds(2 * z, 2)],
            send_sem=send_sem.at[0],
            recv_sem=recv_sem.at[0],
            device_id=zpeer(d),
            device_id_type=MESH,
        )

    def copyk(d):
        return pltpu.make_async_remote_copy(
            src_ref=krow,
            dst_ref=recvk.at[z],
            send_sem=send_sem.at[1],
            recv_sem=recv_sem.at[1],
            device_id=zpeer(d),
            device_id_type=MESH,
        )

    def send1(d, carry):
        copy1(d).start()
        copyk(d).start()
        return carry

    lax.fori_loop(1, NZ, send1, 0)
    recv1[pl.ds(2 * z, 2)] = msg1[z]
    recvk[z] = krow[...]

    loads[5].wait()
    count = band_ref[lat]
    rows = z * T + lax.broadcasted_iota(jnp.int32, (T, 1), 0)
    valid = (rows < count).astype(F32)
    masked = (cot_v[...].astype(F32) * valid).astype(BF16)
    loads[6].wait()
    head_grads = dot(masked, ow_v[...], 1, 1)
    for q in range(8):
        two = head_grads[:, 128 * q : 128 * q + 128]
        hmsg[2 * q] = jnp.where(lane32 < 64, two, 0.0).astype(BF16)
        hmsg[2 * q + 1] = jnp.where(lane32 < 64, pltpu.roll(two, 64, 1), 0.0).astype(BF16)

    def plane_copy(src, dst, slot):
        def make(d):
            chip = lax.rem(p + d, NP)
            return pltpu.make_async_remote_copy(
                src_ref=src(chip),
                dst_ref=dst,
                send_sem=send_sem.at[slot],
                recv_sem=recv_sem.at[slot],
                device_id=plane_peer(chip),
                device_id_type=MESH,
            )

        return make

    def send_all(make):
        def body(d, carry):
            make(d).start()
            return carry

        lax.fori_loop(1, NP, body, 0)

    def whole(ref, slot):
        return pltpu.make_async_remote_copy(
            src_ref=ref,
            dst_ref=ref,
            send_sem=send_sem.at[slot],
            recv_sem=recv_sem.at[slot],
            device_id=zpeer(1),
            device_id_type=MESH,
        )

    send_all(plane_copy(lambda chip: hmsg.at[chip], recvh.at[p], 2))
    recvh[p] = hmsg[p]

    whole(recv1.at[pl.ds(0, 30)], 0).wait_recv()
    whole(recvk.at[pl.ds(0, 15)], 1).wait_recv()
    key_parts = []
    for v in range(V):
        mm[v] = recv1[slots[v]]
        row = recvk[slots[v] // 2]
        first = 16 * lax.rem(slots[v], 2)
        key_parts.append(
            jnp.sum(jnp.where(lane16 == row16 + first, row, 0.0), axis=1, keepdims=True)
        )
    key_rows = jnp.stack(key_parts)
    turned = mm[pl.ds(0, V)].reshape(VK, 128).astype(F32).T
    tmsg[...] = turned[64:128].astype(BF16).reshape(2, 32, VK)
    send_all(plane_copy(lambda chip: tmsg.at[0], recvf.at[p], 3))
    send_all(plane_copy(lambda chip: tmsg.at[1], recvp.at[p], 4))
    recvf[p] = tmsg[0]
    recvp[p] = tmsg[1]

    whole(recvf.at[pl.ds(0, 15)], 3).wait_recv()
    pixels = recvf[...].reshape(TOK, VK).astype(F32).T.reshape(V, K, TOK)
    scores = jnp.sum(pixels * key_rows, axis=1) + key_bias
    exponent = jnp.exp(scores)
    attention = exponent / jnp.sum(exponent, axis=0, keepdims=True)
    weighted = pixels * attention[:, None, :]
    aa[pl.ds(0, VK)] = weighted.reshape(VK, TOK).astype(BF16)
    aa[pl.ds(VK, V)] = attention.astype(BF16)
    whole(recvh.at[pl.ds(0, 15)], 2).wait_recv()
    grads = recvh[...].reshape(TOK, 128)
    head_weights = mm[...].reshape(VK + V, 128)
    lhs = aa[...]
    sums = dot(lhs, grads)
    cross = dot(head_weights, grads, 1, 1)
    dweights = jnp.sum(pixels * cross[0:VK].reshape(V, K, TOK), axis=1) + cross[VK : VK + V]
    dscores = attention * (
        dweights - jnp.sum(attention * dweights, axis=0, keepdims=True)
    )
    score_sums = jnp.sum(pixels * dscores[:, None, :], axis=2, keepdims=True)
    score_rows = jnp.sum(jnp.where(lane16 == 64 + row16, score_sums, 0.0), axis=1)
    dense = sums[0:128] + pltpu.roll(sums[128:256], 64, 1)
    gtile[pl.ds(0, 8)] = dense.astype(BF16).reshape(8, 16, 128)
    gtile[8] = (sums[VK : VK + V] + score_rows).astype(BF16)

    own_slot = 2 * z + core
    even = (lax.rem(z, 2) == 0) & (core == lax.rem(z // 2, 2))
    last = (z == 7) & (core == 0)
    own_tile = jnp.where(even, z // 2, TILES - 1)
    owns = even | last

    def send_tile(i, carry):
        to_z = jnp.where(i == TILES - 1, 7, 2 * i)
        to_core = jnp.where(i == TILES - 1, 0, lax.rem(i, 2))
        here = (to_z == z) & (to_core == core)

        @pl.when(jnp.logical_not(here))
        def _():
            pltpu.make_async_remote_copy(
                src_ref=gtile.at[i],
                dst_ref=recvr.at[own_slot],
                send_sem=send_sem.at[5],
                recv_sem=recv_sem.at[5],
                device_id={"var": to_z, "lat": p * 2 + to_core},
                device_id_type=MESH,
            ).start()

        return carry

    lax.fori_loop(0, TILES, send_tile, 0)

    def copy_total(d):
        there = lax.rem(own_slot + d, 2 * NZ)
        return pltpu.make_async_remote_copy(
            src_ref=red,
            dst_ref=gtot.at[own_tile],
            send_sem=send_sem.at[6],
            recv_sem=recv_sem.at[6],
            device_id={"var": there // 2, "lat": p * 2 + lax.rem(there, 2)},
            device_id_type=MESH,
        )

    @pl.when(owns)
    def _():
        recvr[own_slot] = gtile[own_tile]
        whole(recvr.at[pl.ds(0, 31)], 5).wait_recv()
        total = jnp.sum(recvr[...].astype(F32), axis=0).astype(BF16)
        red[...] = total
        gtot[own_tile] = total

        def body(d, carry):
            copy_total(d).start()
            return carry

        lax.fori_loop(1, 2 * NZ, body, 0)

    pooled = dot(lhs, head_weights, 0, 0)
    pmsg[...] = pooled.astype(BF16).reshape(NP, T, 128)
    send_all(plane_copy(lambda chip: pmsg.at[chip], recvpool.at[p], 7))
    recvpool[p] = pmsg[p]
    bias_rows = pwve[pl.ds(32, 16)]
    whole(recvpool.at[pl.ds(0, 15)], 7).wait_recv()
    parts = []
    for q in range(8):
        left = recvpool[2 * q].astype(F32)
        right = recvpool[2 * q + 1].astype(F32)
        parts.append(jnp.where(lane32 < 64, left, pltpu.roll(right, 64, 1)).astype(BF16))
    projected = dot(jnp.concatenate(parts, axis=1), ow_v[...])
    agg_ref[...] = (projected * valid).astype(BF16)

    whole(recvp.at[pl.ds(0, 15)], 4).wait_recv()

    @pl.when(owns)
    def _():
        whole(gtot.at[pl.ds(0, TILES - 1)], 6).wait_recv()

    @pl.when(jnp.logical_not(owns))
    def _():
        whole(gtot, 6).wait_recv()

    rows_all = recvp[...].reshape(TOK, VK)
    patch_sums = gtot[pl.ds(0, 8)].reshape(128, 128)
    bias_sums = gtot[8]
    low = dot(rows_all[:, 0:128], patch_sums)
    high = dot(rows_all[:, 128:256], patch_sums)
    bias_all = dot(bias_rows, bias_sums, 0, 0).reshape(NP, 2, T, 128)
    bias = jnp.where(core == 0, bias_all[:, 0], bias_all[:, 1])
    value_rows = (low + pltpu.roll(high, 64, 1)).reshape(NP, T, 128) + bias
    picked, score_parts = [], []
    for s in range(2):
        var_of, has = held[s]
        tile = gtot[lax.rem(var_of, 8)].astype(F32)
        tile = jnp.where(var_of < 8, pltpu.roll(tile, 64, 1), tile)
        picked.append(tile * has.astype(F32))
        line = jnp.where((row16 == var_of) & (lane16 >= 64) & (lane16 < 80), bias_sums.astype(F32), 0.0)
        line = jnp.sum(line, axis=0, keepdims=True) * has.astype(F32)
        score_parts.append(pltpu.roll(line, 64 + 16 * s, 1))
    mine = jnp.concatenate(picked, axis=0)
    srow[...] = score_parts[0] + score_parts[1]
    msg5[...] = jnp.where(lane32 < 64, value_rows, mine).astype(BF16)
    send_all(plane_copy(lambda chip: msg5.at[chip], recv5.at[p], 8))
    send_all(plane_copy(lambda chip: srow, recvs.at[p], 9))
    recv5[p] = msg5[p]
    recvs[p] = srow[...]

    loads[7].wait()
    whole(recv5.at[pl.ds(0, 15)], 8).wait_recv()
    whole(recvs.at[pl.ds(0, 15)], 9).wait_recv()
    parts = []
    for q in range(8):
        left = recv5[2 * q].astype(F32)
        right = recv5[2 * q + 1].astype(F32)
        dvw_ref[:, 128 * q : 128 * q + 128] = jnp.where(
            lane32 < 64, left, pltpu.roll(right, 64, 1)
        )
        parts.append(jnp.where(lane32 < 64, pltpu.roll(left, 64, 1), right).astype(BF16))
    patch_grad = dot(jnp.concatenate(parts, axis=1), vw_v[...], 1, 1)
    score_grad = recvs[...].reshape(NP, 128).T[0:32].astype(BF16)
    dpw_ref[...] = patch_grad + dot(score_grad, kq_v[...], 1, 1)

    whole(recv1.at[pl.ds(0, 30)], 0).wait_send()
    whole(recvk.at[pl.ds(0, 15)], 1).wait_send()
    whole(recvh.at[pl.ds(0, 15)], 2).wait_send()
    whole(recvf.at[pl.ds(0, 15)], 3).wait_send()
    whole(recvp.at[pl.ds(0, 15)], 4).wait_send()
    whole(recvpool.at[pl.ds(0, 15)], 7).wait_send()
    whole(recv5.at[pl.ds(0, 15)], 8).wait_send()
    whole(recvs.at[pl.ds(0, 15)], 9).wait_send()

    @pl.when(owns)
    def _():
        whole(gtot.at[pl.ds(0, TILES - 1)], 5).wait_send()
        whole(recvr.at[pl.ds(0, 31)], 6).wait_send()

    @pl.when(jnp.logical_not(owns))
    def _():
        whole(gtot, 5).wait_send()


def per_device(
    fields,
    owner_table,
    band_tokens,
    patch_weight,
    var_embed,
    key_query,
    value_weight,
    out_weight,
    cotangent,
):
    any_spec = pl.BlockSpec(memory_space=pl.ANY)
    smem_spec = pl.BlockSpec(memory_space=pltpu.SMEM)
    vmem_spec = pl.BlockSpec(memory_space=pltpu.VMEM)
    aggregated, value_grad, patch_grad = pl.pallas_call(
        pooling_kernel,
        out_shape=(
            jax.ShapeDtypeStruct((T, D), BF16),
            jax.ShapeDtypeStruct((32, D), F32),
            jax.ShapeDtypeStruct((32, D), F32),
        ),
        in_specs=[smem_spec] * 2 + [any_spec] * 7,
        out_specs=(vmem_spec, vmem_spec, vmem_spec),
        scratch_shapes=[
            pltpu.VMEM((2, K, 512), BF16),
            pltpu.VMEM((48, D), BF16),
            pltpu.VMEM((D, 16), BF16),
            pltpu.VMEM((D, 128), BF16),
            pltpu.VMEM((D, D), BF16),
            pltpu.VMEM((D, D), BF16),
            pltpu.VMEM((T, D), BF16),
            pltpu.VMEM((NZ, 2, K, 128), BF16),
            pltpu.VMEM((2 * NZ, K, 128), BF16),
            pltpu.VMEM((1, 128), F32),
            pltpu.VMEM((NZ, 1, 128), F32),
            pltpu.VMEM((NP, T, 128), BF16),
            pltpu.VMEM((NP, T, 128), BF16),
            pltpu.VMEM((V + 1, K, 128), BF16),
            pltpu.VMEM((2, T, VK), BF16),
            pltpu.VMEM((NP, T, VK), BF16),
            pltpu.VMEM((NP, T, VK), BF16),
            pltpu.VMEM((VK + V, TOK), BF16),
            pltpu.VMEM((NP, T, 128), BF16),
            pltpu.VMEM((NP, T, 128), BF16),
            pltpu.VMEM((TILES, 16, 128), BF16),
            pltpu.VMEM((2 * NZ, 16, 128), BF16),
            pltpu.VMEM((16, 128), BF16),
            pltpu.VMEM((TILES, 16, 128), BF16),
            pltpu.VMEM((NP, T, 128), BF16),
            pltpu.VMEM((NP, T, 128), BF16),
            pltpu.VMEM((1, 128), F32),
            pltpu.VMEM((NP, 1, 128), F32),
            pltpu.SemaphoreType.DMA((8,)),
            pltpu.SemaphoreType.DMA((10,)),
            pltpu.SemaphoreType.DMA((10,)),
        ],
        compiler_params=pltpu.CompilerParams(
            collective_id=0, has_side_effects=True, vmem_limit_bytes=32 * 1024 * 1024
        ),
        cost_estimate=pl.CostEstimate(
            flops=2_000_000_000, bytes_accessed=5_000_000, transcendentals=8192
        ),
    )(
        owner_table,
        band_tokens,
        fields,
        patch_weight.reshape(32, D),
        var_embed,
        key_query,
        value_weight,
        out_weight,
        cotangent.reshape(T, D),
    )
    return (
        aggregated.reshape(1, T, D),
        value_grad,
        patch_grad.reshape(2, K, D),
    )


def solution(mesh):
    in_specs = (
        P("var", None, "lat"),
        P(),
        P(),
        P("var", None, None),
        P(),
        P(),
        P(),
        P(),
        P("lat", "var", None),
    )
    out_specs = (P("lat", "var", None), P("lat", None), P("var", None, None))
    return jax.shard_map(
        per_device, mesh=mesh, in_specs=in_specs, out_specs=out_specs, check_vma=False
    )
```

time: 551 us -> 69.4 us (0.13)
  the two profiles are of different devices: /device:TPU:1 before, /device:TPU:8 now
where the time goes in v1:
time: 69.4 us; the launch traced here: 68.9 us
  Pallas kernels  57.7 us (83%)
  local copies, waits for them, and re-layouts  10.5 us (15%)
    pallas_call x1, Pallas kernels, per_device(): pl.pallas_call(pooling_kernel, out_shape=(jax.ShapeDtypeStruct((T, D), BF...  57.7 us
    unnamed x20, local copies, waits for them, and re-layouts  10.5 us

profile of v1, /device:TPU:8, one launch (start us, length us, event | category | flops | bytes accessed | tf_op | source)
XLA Modules:
  0.0 68.9 jit_solution(15154155133850203750)
XLA Ops:
  0.6 0.9 %copy.12.kq_hbm = bf16[1024,16]{1,0:T(8,128)(2,1)S(1)} copy(bf16[1024,16]{0,1:T(8,128)(2,1)} %param.14) | data formatting | bytes 65536 | tf_op args[5]
  1.6 0.0 copy-start
  1.6 1.6 %copy-done = bf16[1024,1024]{1,0:T(8,128)(2,1)S(1)} copy-done((bf16[1024,1024]{1,0:T(8,128)(2,1)S(1)}, bf16[1024,1024]{1,0:T(8,128)(2,1)}, u32[]{:S(2)}) %copy-start) | copy-done | bytes 2097176
  3.2 0.0 copy-start.1
  3.2 1.6 %copy-done.1 = bf16[1024,1024]{1,0:T(8,128)(2,1)S(1)} copy-done((bf16[1024,1024]{1,0:T(8,128)(2,1)S(1)}, bf16[1024,1024]{1,0:T(8,128)(2,1)}, u32[]{:S(2)}) %copy-start.1) | copy-done | bytes 2097176
  4.8 0.0 copy-start.2
  4.8 0.8 %copy-done.2 = bf16[2,16,1024]{2,1,0:T(8,128)(2,1)S(1)} copy-done((bf16[2,16,1024]{2,1,0:T(8,128)(2,1)S(1)}, bf16[2,16,1024]{2,1,0:T(8,128)(2,1)}, u32[]{:S(2)}) %copy-start.2) | copy-done | bytes 65560
  5.6 0.0 copy-start.3
  5.6 0.8 %copy-done.3 = bf16[1,32,1024]{2,1,0:T(8,128)(2,1)S(1)} copy-done((bf16[1,32,1024]{2,1,0:T(8,128)(2,1)S(1)}, bf16[1,32,1024]{2,1,0:T(8,128)(2,1)}, u32[]{:S(2)}) %copy-start.3) | copy-done | bytes 65560
  6.4 0.0 copy-start.4
  6.4 0.8 %copy-done.4 = bf16[2,16,512]{2,1,0:T(8,128)(2,1)S(1)} copy-done((bf16[2,16,512]{2,1,0:T(8,128)(2,1)S(1)}, bf16[2,16,512]{2,1,0:T(8,128)(2,1)}, u32[]{:S(2)}) %copy-start.4) | copy-done | bytes 32792
  7.2 0.0 copy-start.5
  7.2 0.8 %copy-done.5 = bf16[16,1024]{1,0:T(8,128)(2,1)S(1)} copy-done((bf16[16,1024]{1,0:T(8,128)(2,1)S(1)}, bf16[16,1024]{1,0:T(8,128)(2,1)}, u32[]{:S(2)}) %copy-start.5) | copy-done | bytes 32792
  7.9 0.0 copy-start.6
  7.9 0.7 copy-done.6
  8.6 0.0 copy-start.7
  8.6 0.7 copy-done.7
  9.3 57.7 %shard_map.112 = (bf16[32,1024]{1,0:T(8,128)(2,1)S(1)}, f32[32,1024]{1,0:T(8,128)S(1)}, f32[32,1024]{1,0:T(8,128)S(1)}) custom-call(s32[16]{0:T(128)S(1)} %copy-done.6, s32[32]{0:T(128)S(1)} %copy-done.7, bf16[2,16,512]{2,1,0:T(8,128)(2,1)S(1)} %copy-done.4, bf16[32,1024]{1,0:T(8,128)(2,1)S(1)} %bitcast.6, bf16[16,1024]{1,0:T(8,128)(2,1)S(1)} %copy-done.5, ...), custom_call_target="tpu_custom_call" | custom-call | flops 2000000000 | bytes 5000000 | tf_op jit(solution)/shard_map/pallas_call | solution.py:429
  67.0 0.6 copy.16
  67.6 0.7 copy.17
  68.2 0.7 copy.18
Async XLA Ops:
  1.6 1.6 %copy-start = (bf16[1024,1024]{1,0:T(8,128)(2,1)S(1)}, bf16[1024,1024]{1,0:T(8,128)(2,1)}, u32[]{:S(2)}) copy-start(bf16[1024,1024]{1,0:T(8,128)(2,1)} %vw_hbm.1) | copy-start | bytes 6291460
  3.2 1.6 %copy-start.1 = (bf16[1024,1024]{1,0:T(8,128)(2,1)S(1)}, bf16[1024,1024]{1,0:T(8,128)(2,1)}, u32[]{:S(2)}) copy-start(bf16[1024,1024]{1,0:T(8,128)(2,1)} %ow_hbm.1) | copy-start | bytes 6291460
  4.8 0.8 %copy-start.2 = (bf16[2,16,1024]{2,1,0:T(8,128)(2,1)S(1)}, bf16[2,16,1024]{2,1,0:T(8,128)(2,1)}, u32[]{:S(2)}) copy-start(bf16[2,16,1024]{2,1,0:T(8,128)(2,1)} %param.12) | copy-start | bytes 196612
  5.6 0.8 %copy-start.3 = (bf16[1,32,1024]{2,1,0:T(8,128)(2,1)S(1)}, bf16[1,32,1024]{2,1,0:T(8,128)(2,1)}, u32[]{:S(2)}) copy-start(bf16[1,32,1024]{2,1,0:T(8,128)(2,1)} %param.17) | copy-start | bytes 196612
  6.4 0.8 %copy-start.4 = (bf16[2,16,512]{2,1,0:T(8,128)(2,1)S(1)}, bf16[2,16,512]{2,1,0:T(8,128)(2,1)}, u32[]{:S(2)}) copy-start(bf16[2,16,512]{2,1,0:T(8,128)(2,1)} %fields_hbm.1) | copy-start | bytes 98308
  7.2 0.8 %copy-start.5 = (bf16[16,1024]{1,0:T(8,128)(2,1)S(1)}, bf16[16,1024]{1,0:T(8,128)(2,1)}, u32[]{:S(2)}) copy-start(bf16[16,1024]{1,0:T(8,128)(2,1)} %ve_hbm.1) | copy-start | bytes 98308
  7.9 0.7 copy-start.6
  8.6 0.7 copy-start.7

commit v2 on v1

v2 whole, which is shorter than its diff:
```python
import functools

import jax
import jax.numpy as jnp
from jax import lax
from jax.experimental import pallas as pl
from jax.experimental.pallas import tpu as pltpu
from jax.sharding import PartitionSpec as P

MESH = pl.DeviceIdType.MESH
F32 = jnp.float32
BF16 = jnp.bfloat16

NZ = 16
NP = 16
V = 16
K = 16
T = 32
D = 1024
TILES = 9
FAR_FIRST = (8, 7, 9, 6, 10, 5, 11, 4, 12, 3, 13, 2, 14, 1, 15)
PLANE_STEPS = sorted(
    [(dx, dy) for dx in range(4) for dy in range(4) if dx or dy],
    key=lambda step: -sum(min(d, 4 - d) for d in step),
)
VK = V * K
TOK = NP * T


def dot(a, b, ca=1, cb=0):
    return lax.dot_general(a, b, (((ca,), (cb,)), ((), ())), preferred_element_type=F32)


def pooling_kernel(
    owner_ref,
    band_ref,
    fields_hbm,
    pw_hbm,
    ve_hbm,
    kq_hbm,
    vw_hbm,
    ow_hbm,
    cot_hbm,
    agg_ref,
    dvw_ref,
    dpw_ref,
    fields_v,
    pwve,
    kq_v,
    vwg,
    vw_v,
    ow_v,
    cot_v,
    fmsg,
    recv0,
    wmsg,
    recv1,
    hmsg,
    recvh,
    mm,
    fturn,
    pturn,
    recvf,
    recvp,
    aa,
    pmsg,
    recvpool,
    gtile,
    recvr,
    recvb,
    quad,
    quadb,
    recvq,
    recvqb,
    gtot,
    msg5,
    recv5,
    srow,
    recvs,
    load_sem,
    send_sem,
    recv_sem,
):
    z = lax.axis_index("var")
    lat = lax.axis_index("lat")
    core = lax.rem(lat, 2)
    p = lat // 2

    x, y = p // 4, lax.rem(p, 4)
    sibling = {"var": z, "lat": p * 2 + 1 - core}

    def zpeer(d):
        return {"var": lax.rem(z + d, NZ), "lat": lat}

    def plane_chip(step):
        return lax.rem(x + step[0], 4) * 4 + lax.rem(y + step[1], 4)

    def plane_peer(chip):
        return {"var": z, "lat": chip * 2 + core}

    def quad_device(j):
        return {"var": (z // 4) * 4 + lax.rem(j, 4), "lat": p * 2 + j // 4}

    barrier = pltpu.get_barrier_semaphore()

    def signal(device):
        pl.semaphore_signal(barrier, inc=1, device_id=device, device_id_type=MESH)

    own_j = core * 4 + lax.rem(z, 4)
    for d in FAR_FIRST:
        signal(zpeer(d))
    for step in PLANE_STEPS:
        signal(plane_peer(plane_chip(step)))
    signal(sibling)
    for d in range(1, 4):
        other = (z // 4) * 4 + lax.rem(z + d, 4)
        signal({"var": other, "lat": p * 2 + 1 - core})

    def whole(ref, slot):
        return pltpu.make_async_remote_copy(
            src_ref=ref,
            dst_ref=ref,
            send_sem=send_sem.at[slot],
            recv_sem=recv_sem.at[slot],
            device_id=sibling,
            device_id_type=MESH,
        )

    def send(src, dst, slot, device):
        pltpu.make_async_remote_copy(
            src_ref=src,
            dst_ref=dst,
            send_sem=send_sem.at[slot],
            recv_sem=recv_sem.at[slot],
            device_id=device,
            device_id_type=MESH,
        ).start()

    def send_plane(src, dst, slot):
        for step in PLANE_STEPS:
            chip = plane_chip(step)
            send(src(chip), dst, slot, plane_peer(chip))

    group = pl.multiple_of((p // 2) * 128, 128)
    loads = [
        pltpu.make_async_copy(fields_hbm, fields_v, load_sem.at[4]),
        pltpu.make_async_copy(pw_hbm, pwve.at[pl.ds(0, 32)], load_sem.at[0]),
        pltpu.make_async_copy(ve_hbm, pwve.at[pl.ds(32, 16)], load_sem.at[1]),
        pltpu.make_async_copy(vw_hbm.at[:, pl.ds(group, 128)], vwg, load_sem.at[2]),
        pltpu.make_async_copy(kq_hbm, kq_v, load_sem.at[3]),
        pltpu.make_async_copy(cot_hbm, cot_v, load_sem.at[5]),
        pltpu.make_async_copy(ow_hbm, ow_v, load_sem.at[6]),
        pltpu.make_async_copy(vw_hbm, vw_v, load_sem.at[7]),
    ]
    for load in loads:
        load.start()

    owners = [owner_ref[v] for v in range(V)]
    slots = []
    for v in range(V):
        rank = jnp.int32(0)
        for u in range(v):
            rank = rank + (owners[u] == owners[v]).astype(jnp.int32)
        slots.append(owners[v] * 2 + rank)
    held = []
    for s in range(2):
        var_of, has = jnp.int32(0), jnp.int32(0)
        for v in range(V):
            hit = (slots[v] == 2 * z + s).astype(jnp.int32)
            var_of, has = var_of + hit * v, has + hit
        held.append((var_of, has))

    lane16 = lax.broadcasted_iota(jnp.int32, (16, 128), 1)
    row16 = lax.broadcasted_iota(jnp.int32, (16, 128), 0)
    lane32 = lax.broadcasted_iota(jnp.int32, (32, 128), 1)
    row32 = lax.broadcasted_iota(jnp.int32, (32, 128), 0)

    loads[0].wait()
    for q in range(4):
        low = fields_v[0, :, 128 * q : 128 * q + 128].astype(F32)
        high = fields_v[1, :, 128 * q : 128 * q + 128].astype(F32)
        for r in range(4):
            left = pltpu.roll(low, (128 - 32 * r) % 128, 1) if r else low
            right = pltpu.roll(high, (160 - 32 * r) % 128, 1) if r != 1 else high
            piece = jnp.where(lane16 < 32, left, jnp.where(lane16 < 64, right, 0.0))
            fmsg[4 * q + r] = piece.astype(BF16)

    for i in range(1, 5):
        loads[i].wait()
    turn = lax.rem(p, 2) * 64
    both = pwve[...]
    head_cols = pltpu.roll(dot(both, vwg[...]), turn, 1)
    key_cols = dot(both, kq_v[...], 1, 1)
    key_lane = lax.broadcasted_iota(jnp.int32, (48, 16), 1)
    key_col = jnp.sum(jnp.where(key_lane == p, key_cols, 0.0), axis=1, keepdims=True)
    key_bias = key_col[32:48]
    mm[V] = jnp.where(lane16 < 64, head_cols[32:48], 0.0).astype(BF16)
    own_group = pl.multiple_of((lat // 4) * 128, 128)
    own_cols = pltpu.roll(
        pwve[pl.ds(0, 32), pl.ds(own_group, 128)].astype(F32),
        lax.rem(192 - 32 * lax.rem(lat, 4), 128),
        1,
    )
    key_top = key_col[0:32].astype(BF16).astype(F32)
    key_mid = (key_col[0:32] - key_top).astype(BF16).astype(F32)
    key_low = key_col[0:32] - key_top - key_mid
    packed = jnp.where(lane32 < 64, head_cols[0:32], own_cols)
    packed = jnp.where(lane32 < 96, packed, jnp.where(lane32 == 96, key_top, 0.0))
    packed = jnp.where(lane32 == 97, key_mid, jnp.where(lane32 == 98, key_low, packed))
    wmsg[...] = packed.astype(BF16).reshape(2, 16, 128)

    pl.semaphore_wait(barrier, 34)

    for d in FAR_FIRST:
        send(fmsg.at[lax.rem(z + d, NZ)], recv0.at[z], 0, zpeer(d))
    for d in FAR_FIRST:
        send(wmsg, recv1.at[pl.ds(2 * z, 2)], 1, zpeer(d))
    recv0[z] = fmsg[z]
    recv1[pl.ds(2 * z, 2)] = wmsg[...]

    loads[5].wait()
    count = band_ref[lat]
    rows = z * T + lax.broadcasted_iota(jnp.int32, (T, 1), 0)
    valid = (rows < count).astype(F32)
    masked = (cot_v[...].astype(F32) * valid).astype(BF16)
    loads[6].wait()
    head_grads = dot(masked, ow_v[...], 1, 1)
    for q in range(8):
        two = head_grads[:, 128 * q : 128 * q + 128]
        hmsg[2 * q] = jnp.where(lane32 < 64, two, 0.0).astype(BF16)
        hmsg[2 * q + 1] = jnp.where(lane32 < 64, pltpu.roll(two, 64, 1), 0.0).astype(BF16)

    send_plane(lambda chip: hmsg.at[chip], recvh.at[p], 2)
    recvh[p] = hmsg[p]

    whole(recv0.at[pl.ds(0, 15)], 0).wait_recv()
    pieces = []
    for v in range(V):
        tile = recv0[slots[v] // 2].astype(F32)
        pieces.append(pltpu.roll(tile, lax.rem(128 - 32 * lax.rem(slots[v], 2), 128), 1))
    fturn[...] = jnp.concatenate(pieces, axis=0).T[0:32].astype(BF16)
    send_plane(lambda chip: fturn, recvf.at[p], 3)
    recvf[p] = fturn[...]

    whole(recv1.at[pl.ds(0, 30)], 1).wait_recv()
    for v in range(V):
        mm[v] = recv1[slots[v]]
    chosen = mm[pl.ds(0, V)].reshape(VK, 128).astype(F32)
    lane_all = lax.broadcasted_iota(jnp.int32, (VK, 128), 1)
    key_rows = jnp.sum(
        jnp.where((lane_all >= 96) & (lane_all < 99), chosen, 0.0), axis=1, keepdims=True
    ).reshape(V, K, 1)
    pturn[...] = chosen.T[64:96].astype(BF16)

    whole(recvf.at[pl.ds(0, 15)], 3).wait_recv()
    pixels = recvf[...].reshape(TOK, VK).astype(F32).T.reshape(V, K, TOK)
    scores = jnp.sum(pixels * key_rows, axis=1) + key_bias
    exponent = jnp.exp(scores)
    attention = exponent / jnp.sum(exponent, axis=0, keepdims=True)
    weighted = pixels * attention[:, None, :]
    aa[pl.ds(0, VK)] = weighted.reshape(VK, TOK).astype(BF16)
    aa[pl.ds(VK, V)] = attention.astype(BF16)
    whole(recvh.at[pl.ds(0, 15)], 2).wait_recv()
    grads = recvh[...].reshape(TOK, 128)
    head_weights = mm[...].reshape(VK + V, 128)
    lhs = aa[...]
    sums = dot(lhs, grads)
    cross = dot(head_weights, grads, 1, 1)
    dweights = jnp.sum(pixels * cross[0:VK].reshape(V, K, TOK), axis=1) + cross[VK : VK + V]
    dscores = attention * (
        dweights - jnp.sum(attention * dweights, axis=0, keepdims=True)
    )
    score_sums = jnp.sum(pixels * dscores[:, None, :], axis=2, keepdims=True)
    score_rows = jnp.sum(jnp.where(lane16 == 64 + row16, score_sums, 0.0), axis=1)
    dense = sums[0:128] + pltpu.roll(sums[128:256], 64, 1)
    gtile[pl.ds(0, 8)] = dense.astype(BF16).reshape(8, 16, 128)
    gtile[8] = (sums[VK : VK + V] + score_rows).astype(BF16)

    for d in range(1, 8):
        j = lax.rem(own_j + d, 8)
        send(gtile.at[j], recvr.at[own_j], 5, quad_device(j))
    recvr[own_j] = gtile[own_j]
    has_bias = own_j == 1

    @pl.when(has_bias)
    def _():
        recvb[own_j] = gtile[8]

    @pl.when(jnp.logical_not(has_bias))
    def _():
        send(gtile.at[8], recvb.at[own_j], 6, quad_device(jnp.int32(1)))

    pooled = dot(lhs, head_weights, 0, 0)
    pmsg[...] = pooled.astype(BF16).reshape(NP, T, 128)
    send_plane(lambda chip: pmsg.at[chip], recvpool.at[p], 7)
    recvpool[p] = pmsg[p]
    send_plane(lambda chip: pturn, recvp.at[p], 4)
    recvp[p] = pturn[...]

    whole(recvr.at[pl.ds(0, 7)], 5).wait_recv()
    quad[...] = jnp.sum(recvr[...].astype(F32), axis=0).astype(BF16)
    for d in FAR_FIRST:
        send(quad, recvq.at[z], 10, zpeer(d))
    recvq[z] = quad[...]

    @pl.when(has_bias)
    def _():
        whole(recvb.at[pl.ds(0, 7)], 6).wait_recv()
        quadb[...] = jnp.sum(recvb[...].astype(F32), axis=0).astype(BF16)
        for d in FAR_FIRST:
            send(quadb, recvqb.at[z // 4], 11, zpeer(d))
        recvqb[z // 4] = quadb[...]

    bias_rows = pwve[pl.ds(32, 16)]
    whole(recvpool.at[pl.ds(0, 15)], 7).wait_recv()
    parts = []
    for q in range(8):
        left = recvpool[2 * q].astype(F32)
        right = recvpool[2 * q + 1].astype(F32)
        parts.append(jnp.where(lane32 < 64, left, pltpu.roll(right, 64, 1)).astype(BF16))
    projected = dot(jnp.concatenate(parts, axis=1), ow_v[...])
    agg_ref[...] = (projected * valid).astype(BF16)

    whole(recvp.at[pl.ds(0, 15)], 4).wait_recv()
    whole(recvq.at[pl.ds(0, 15)], 10).wait_recv()
    half = jnp.sum(recvq[...].astype(F32).reshape(4, 4, 16, 128), axis=0).astype(BF16)
    half_at = pl.multiple_of(5 * core, 5)
    gtot[pl.ds(half_at, 4)] = half

    @pl.when(core == 1)
    def _():
        gtot[9] = jnp.zeros((16, 128), BF16)

    @pl.when((core == 0) & has_bias)
    def _():
        whole(recvqb.at[pl.ds(0, 3)], 11).wait_recv()

    @pl.when((core == 0) & jnp.logical_not(has_bias))
    def _():
        whole(recvqb, 11).wait_recv()

    @pl.when(core == 0)
    def _():
        gtot[4] = jnp.sum(recvqb[...].astype(F32), axis=0).astype(BF16)

    send(gtot.at[pl.ds(half_at, 5)], gtot.at[pl.ds(half_at, 5)], 12, sibling)
    whole(gtot.at[pl.ds(0, 5)], 12).wait_recv()

    rows_all = recvp[...].reshape(TOK, VK)
    patch_sums = jnp.concatenate([gtot[pl.ds(0, 4)], gtot[pl.ds(5, 4)]], axis=0).reshape(128, 128)
    bias_sums = gtot[4]
    low = dot(rows_all[:, 0:128], patch_sums)
    high = dot(rows_all[:, 128:256], patch_sums)
    bias_all = dot(bias_rows, bias_sums, 0, 0).reshape(NP, 2, T, 128)
    bias = jnp.where(core == 0, bias_all[:, 0], bias_all[:, 1])
    value_rows = (low + pltpu.roll(high, 64, 1)).reshape(NP, T, 128) + bias
    picked, score_parts = [], []
    for s in range(2):
        var_of, has = held[s]
        at = lax.rem(var_of, 8)
        tile = gtot[at + at // 4].astype(F32)
        tile = jnp.where(var_of < 8, pltpu.roll(tile, 64, 1), tile)
        picked.append(tile * has.astype(F32))
        line = jnp.where((row16 == var_of) & (lane16 >= 64) & (lane16 < 80), bias_sums.astype(F32), 0.0)
        line = jnp.sum(line, axis=0, keepdims=True) * has.astype(F32)
        score_parts.append(pltpu.roll(line, 64 + 16 * s, 1))
    mine = jnp.concatenate(picked, axis=0)
    srow[...] = score_parts[0] + score_parts[1]
    msg5[...] = jnp.where(lane32 < 64, value_rows, mine).astype(BF16)
    send_plane(lambda chip: msg5.at[chip], recv5.at[p], 8)
    send_plane(lambda chip: srow, recvs.at[p], 9)
    recv5[p] = msg5[p]
    recvs[p] = srow[...]

    loads[7].wait()
    whole(recv5.at[pl.ds(0, 15)], 8).wait_recv()
    whole(recvs.at[pl.ds(0, 15)], 9).wait_recv()
    parts = []
    for q in range(8):
        left = recv5[2 * q].astype(F32)
        right = recv5[2 * q + 1].astype(F32)
        dvw_ref[:, 128 * q : 128 * q + 128] = jnp.where(
            lane32 < 64, left, pltpu.roll(right, 64, 1)
        )
        parts.append(jnp.where(lane32 < 64, pltpu.roll(left, 64, 1), right).astype(BF16))
    patch_grad = dot(jnp.concatenate(parts, axis=1), vw_v[...], 1, 1)
    score_grad = recvs[...].reshape(NP, 128).T[0:32].astype(BF16)
    dpw_ref[...] = patch_grad + dot(score_grad, kq_v[...])

    whole(recv0.at[pl.ds(0, 15)], 0).wait_send()
    whole(recv1.at[pl.ds(0, 30)], 1).wait_send()
    whole(recvh.at[pl.ds(0, 15)], 2).wait_send()
    whole(recvf.at[pl.ds(0, 15)], 3).wait_send()
    whole(recvp.at[pl.ds(0, 15)], 4).wait_send()
    whole(recvr.at[pl.ds(0, 7)], 5).wait_send()
    whole(recvpool.at[pl.ds(0, 15)], 7).wait_send()
    whole(recv5.at[pl.ds(0, 15)], 8).wait_send()
    whole(recvs.at[pl.ds(0, 15)], 9).wait_send()
    whole(recvq.at[pl.ds(0, 15)], 10).wait_send()
    whole(gtot.at[pl.ds(0, 5)], 12).wait_send()

    @pl.when(has_bias)
    def _():
        whole(recvq.at[pl.ds(0, 15)], 11).wait_send()

    @pl.when(jnp.logical_not(has_bias))
    def _():
        whole(quadb, 6).wait_send()


def per_device(
    fields,
    owner_table,
    band_tokens,
    patch_weight,
    var_embed,
    key_query,
    value_weight,
    out_weight,
    cotangent,
):
    hbm_spec = pl.BlockSpec(memory_space=pltpu.HBM)
    smem_spec = pl.BlockSpec(memory_space=pltpu.SMEM)
    vmem_spec = pl.BlockSpec(memory_space=pltpu.VMEM)
    aggregated, value_grad, patch_grad = pl.pallas_call(
        pooling_kernel,
        out_shape=(
            jax.ShapeDtypeStruct((T, D), BF16),
            jax.ShapeDtypeStruct((32, D), F32),
            jax.ShapeDtypeStruct((32, D), F32),
        ),
        in_specs=[smem_spec] * 2 + [hbm_spec] * 7,
        out_specs=(vmem_spec, vmem_spec, vmem_spec),
        scratch_shapes=[
            pltpu.VMEM((2, K, 512), BF16),
            pltpu.VMEM((48, D), BF16),
            pltpu.VMEM((16, D), BF16),
            pltpu.VMEM((D, 128), BF16),
            pltpu.VMEM((D, D), BF16),
            pltpu.VMEM((D, D), BF16),
            pltpu.VMEM((T, D), BF16),
            pltpu.VMEM((NZ, K, 128), BF16),
            pltpu.VMEM((NZ, K, 128), BF16),
            pltpu.VMEM((2, K, 128), BF16),
            pltpu.VMEM((2 * NZ, K, 128), BF16),
            pltpu.VMEM((NP, T, 128), BF16),
            pltpu.VMEM((NP, T, 128), BF16),
            pltpu.VMEM((V + 1, K, 128), BF16),
            pltpu.VMEM((T, VK), BF16),
            pltpu.VMEM((32, VK), BF16),
            pltpu.VMEM((NP, T, VK), BF16),
            pltpu.VMEM((NP, T, VK), BF16),
            pltpu.VMEM((VK + V, TOK), BF16),
            pltpu.VMEM((NP, T, 128), BF16),
            pltpu.VMEM((NP, T, 128), BF16),
            pltpu.VMEM((TILES, 16, 128), BF16),
            pltpu.VMEM((8, 16, 128), BF16),
            pltpu.VMEM((8, 16, 128), BF16),
            pltpu.VMEM((16, 128), BF16),
            pltpu.VMEM((16, 128), BF16),
            pltpu.VMEM((NZ, 16, 128), BF16),
            pltpu.VMEM((4, 16, 128), BF16),
            pltpu.VMEM((10, 16, 128), BF16),
            pltpu.VMEM((NP, T, 128), BF16),
            pltpu.VMEM((NP, T, 128), BF16),
            pltpu.VMEM((1, 128), F32),
            pltpu.VMEM((NP, 1, 128), F32),
            pltpu.SemaphoreType.DMA((8,)),
            pltpu.SemaphoreType.DMA((14,)),
            pltpu.SemaphoreType.DMA((14,)),
        ],
        compiler_params=pltpu.CompilerParams(
            collective_id=0, has_side_effects=True, vmem_limit_bytes=60 * 1024 * 1024
        ),
        cost_estimate=pl.CostEstimate(
            flops=2_000_000_000, bytes_accessed=5_000_000, transcendentals=8192
        ),
    )(
        owner_table,
        band_tokens,
        fields,
        patch_weight.reshape(32, D),
        var_embed,
        key_query.T,
        value_weight,
        out_weight,
        cotangent.reshape(T, D),
    )
    return (
        aggregated.reshape(1, T, D),
        value_grad,
        patch_grad.reshape(2, K, D),
    )


def solution(mesh):
    in_specs = (
        P("var", None, "lat"),
        P(),
        P(),
        P("var", None, None),
        P(),
        P(),
        P(),
        P(),
        P("lat", "var", None),
    )
    out_specs = (P("lat", "var", None), P("lat", None), P("var", None, None))
    return jax.shard_map(
        per_device, mesh=mesh, in_specs=in_specs, out_specs=out_specs, check_vma=False
    )
```

time: 69.4 us -> 58.1 us (0.84)
  the two profiles are of different devices: /device:TPU:8 before, /device:TPU:1 now
where the time goes in v2:
time: 58.1 us; the launch traced here: 57.9 us
  Pallas kernels  52.7 us (91%)
  local copies, waits for them, and re-layouts  4.61 us (8%)
  between operations  0.64 us (1%)
    pallas_call x1, Pallas kernels, per_device(): pl.pallas_call(pooling_kernel, out_shape=(jax.ShapeDtypeStruct((T, D), BF...  52.7 us
    unnamed x3, local copies, waits for them, and re-layouts  4.61 us

profile of v2, /device:TPU:1, one launch (start us, length us, event | category | flops | bytes accessed | tf_op | source)
XLA Modules:
  0.0 57.9 jit_solution(8247619352037785328)
XLA Ops:
  0.6 52.7 %shard_map.112 = (bf16[32,1024]{1,0:T(8,128)(2,1)}, f32[32,1024]{1,0:T(8,128)}, f32[32,1024]{1,0:T(8,128)}) custom-call(s32[16]{0:T(128)} %owner_ref.1, s32[32]{0:T(128)} %band_ref.1, bf16[2,16,512]{2,1,0:T(8,128)(2,1)} %fields_hbm.1, bf16[32,1024]{1,0:T(8,128)(2,1)} %bitcast.7, bf16[16,1024]{1,0:T(8,128)(2,1)} %ve_hbm.1, bf16[16,1024]{1,0:T(8,128)(2,1)} %bitcast.9, ...), custom_call_target="tpu_custom_call" | custom-call | flops 2000000000 | bytes 5000000 | tf_op jit(solution)/shard_map/pallas_call | solution.py:425
  53.3 1.5 %copy.15 = bf16[1,32,1024]{2,1,0:T(8,128)(2,1)} copy(bf16[1,32,1024]{2,1,0:T(8,128)(2,1)} %bitcast.6) | data formatting | bytes 131072
  54.8 1.6 %copy.16 = f32[32,1024]{1,0:T(8,128)} copy(f32[32,1024]{1,0:T(8,128)} %get-tuple-element.13) | data formatting | bytes 262144
  56.3 1.6 %copy.17 = f32[2,16,1024]{2,1,0:T(8,128)} copy(f32[2,16,1024]{2,1,0:T(8,128)} %bitcast.5) | data formatting | bytes 262144

commit v3 on v2

--- a/solution.py
+++ b/solution.py
@@ -32,8 +32,8 @@
 
 
 def pooling_kernel(
-    owner_ref,
-    band_ref,
+    owner_hbm,
+    band_hbm,
     fields_hbm,
     pw_hbm,
     ve_hbm,
@@ -44,6 +44,8 @@
     agg_ref,
     dvw_ref,
     dpw_ref,
+    owner_ref,
+    band_ref,
     fields_v,
     pwve,
     kq_v,
@@ -75,8 +77,6 @@
     gtot,
     msg5,
     recv5,
-    srow,
-    recvs,
     load_sem,
     send_sem,
     recv_sem,
@@ -151,10 +151,26 @@
         pltpu.make_async_copy(cot_hbm, cot_v, load_sem.at[5]),
         pltpu.make_async_copy(ow_hbm, ow_v, load_sem.at[6]),
         pltpu.make_async_copy(vw_hbm, vw_v, load_sem.at[7]),
+        pltpu.make_async_copy(owner_hbm, owner_ref, load_sem.at[8]),
+        pltpu.make_async_copy(band_hbm, band_ref, load_sem.at[9]),
     ]
-    for load in loads:
+    for load in loads[8:] + loads[:8]:
         load.start()
 
+    lane16 = lax.broadcasted_iota(jnp.int32, (16, 128), 1)
+    row16 = lax.broadcasted_iota(jnp.int32, (16, 128), 0)
+    lane32 = lax.broadcasted_iota(jnp.int32, (32, 128), 1)
+    loads[0].wait()
+    for q in range(4):
+        low = fields_v[0, :, 128 * q : 128 * q + 128].astype(F32)
+        high = fields_v[1, :, 128 * q : 128 * q + 128].astype(F32)
+        for r in range(4):
+            left = pltpu.roll(low, (128 - 32 * r) % 128, 1) if r else low
+            right = pltpu.roll(high, (160 - 32 * r) % 128, 1) if r != 1 else high
+            piece = jnp.where(lane16 < 32, left, jnp.where(lane16 < 64, right, 0.0))
+            fmsg[4 * q + r] = piece.astype(BF16)
+
+    loads[8].wait()
     owners = [owner_ref[v] for v in range(V)]
     slots = []
     for v in range(V):
@@ -169,21 +185,6 @@
             hit = (slots[v] == 2 * z + s).astype(jnp.int32)
             var_of, has = var_of + hit * v, has + hit
         held.append((var_of, has))
-
-    lane16 = lax.broadcasted_iota(jnp.int32, (16, 128), 1)
-    row16 = lax.broadcasted_iota(jnp.int32, (16, 128), 0)
-    lane32 = lax.broadcasted_iota(jnp.int32, (32, 128), 1)
-    row32 = lax.broadcasted_iota(jnp.int32, (32, 128), 0)
-
-    loads[0].wait()
-    for q in range(4):
-        low = fields_v[0, :, 128 * q : 128 * q + 128].astype(F32)
-        high = fields_v[1, :, 128 * q : 128 * q + 128].astype(F32)
-        for r in range(4):
-            left = pltpu.roll(low, (128 - 32 * r) % 128, 1) if r else low
-            right = pltpu.roll(high, (160 - 32 * r) % 128, 1) if r != 1 else high
-            piece = jnp.where(lane16 < 32, left, jnp.where(lane16 < 64, right, 0.0))
-            fmsg[4 * q + r] = piece.astype(BF16)
 
     for i in range(1, 5):
         loads[i].wait()
@@ -219,6 +220,7 @@
     recv1[pl.ds(2 * z, 2)] = wmsg[...]
 
     loads[5].wait()
+    loads[9].wait()
     count = band_ref[lat]
     rows = z * T + lax.broadcasted_iota(jnp.int32, (T, 1), 0)
     valid = (rows < count).astype(F32)
@@ -251,6 +253,8 @@
         jnp.where((lane_all >= 96) & (lane_all < 99), chosen, 0.0), axis=1, keepdims=True
     ).reshape(V, K, 1)
     pturn[...] = chosen.T[64:96].astype(BF16)
+    send_plane(lambda chip: pturn, recvp.at[p], 4)
+    recvp[p] = pturn[...]
 
     whole(recvf.at[pl.ds(0, 15)], 3).wait_recv()
     pixels = recvf[...].reshape(TOK, VK).astype(F32).T.reshape(V, K, TOK)
@@ -292,10 +296,6 @@
 
     pooled = dot(lhs, head_weights, 0, 0)
     pmsg[...] = pooled.astype(BF16).reshape(NP, T, 128)
-    send_plane(lambda chip: pmsg.at[chip], recvpool.at[p], 7)
-    recvpool[p] = pmsg[p]
-    send_plane(lambda chip: pturn, recvp.at[p], 4)
-    recvp[p] = pturn[...]
 
     whole(recvr.at[pl.ds(0, 7)], 5).wait_recv()
     quad[...] = jnp.sum(recvr[...].astype(F32), axis=0).astype(BF16)
@@ -311,15 +311,8 @@
             send(quadb, recvqb.at[z // 4], 11, zpeer(d))
         recvqb[z // 4] = quadb[...]
 
-    bias_rows = pwve[pl.ds(32, 16)]
-    whole(recvpool.at[pl.ds(0, 15)], 7).wait_recv()
-    parts = []
-    for q in range(8):
-        left = recvpool[2 * q].astype(F32)
-        right = recvpool[2 * q + 1].astype(F32)
-        parts.append(jnp.where(lane32 < 64, left, pltpu.roll(right, 64, 1)).astype(BF16))
-    projected = dot(jnp.concatenate(parts, axis=1), ow_v[...])
-    agg_ref[...] = (projected * valid).astype(BF16)
+    send_plane(lambda chip: pmsg.at[chip], recvpool.at[p], 7)
+    recvpool[p] = pmsg[p]
 
     whole(recvp.at[pl.ds(0, 15)], 4).wait_recv()
     whole(recvq.at[pl.ds(0, 15)], 10).wait_recv()
@@ -346,6 +339,7 @@
     send(gtot.at[pl.ds(half_at, 5)], gtot.at[pl.ds(half_at, 5)], 12, sibling)
     whole(gtot.at[pl.ds(0, 5)], 12).wait_recv()
 
+    bias_rows = pwve[pl.ds(32, 16)]
     rows_all = recvp[...].reshape(TOK, VK)
     patch_sums = jnp.concatenate([gtot[pl.ds(0, 4)], gtot[pl.ds(5, 4)]], axis=0).reshape(128, 128)
     bias_sums = gtot[4]
@@ -365,26 +359,37 @@
         line = jnp.sum(line, axis=0, keepdims=True) * has.astype(F32)
         score_parts.append(pltpu.roll(line, 64 + 16 * s, 1))
     mine = jnp.concatenate(picked, axis=0)
-    srow[...] = score_parts[0] + score_parts[1]
-    msg5[...] = jnp.where(lane32 < 64, value_rows, mine).astype(BF16)
+    score_line = jnp.broadcast_to(score_parts[0] + score_parts[1], (16, 128)).astype(BF16)
+    msg5[:, 0:32, :] = jnp.where(lane32 < 64, value_rows, mine).astype(BF16)
+    msg5[:, 32:48, :] = jnp.broadcast_to(score_line, (NP, 16, 128))
     send_plane(lambda chip: msg5.at[chip], recv5.at[p], 8)
-    send_plane(lambda chip: srow, recvs.at[p], 9)
     recv5[p] = msg5[p]
-    recvs[p] = srow[...]
+
+    whole(recvpool.at[pl.ds(0, 15)], 7).wait_recv()
+    parts = []
+    for q in range(8):
+        left = recvpool[2 * q].astype(F32)
+        right = recvpool[2 * q + 1].astype(F32)
+        parts.append(jnp.where(lane32 < 64, left, pltpu.roll(right, 64, 1)).astype(BF16))
+    projected = dot(jnp.concatenate(parts, axis=1), ow_v[...])
+    agg_ref[...] = (projected * valid).astype(BF16)
 
     loads[7].wait()
     whole(recv5.at[pl.ds(0, 15)], 8).wait_recv()
-    whole(recvs.at[pl.ds(0, 15)], 9).wait_recv()
     parts = []
     for q in range(8):
-        left = recv5[2 * q].astype(F32)
-        right = recv5[2 * q + 1].astype(F32)
+        left = recv5[2 * q, 0:32].astype(F32)
+        right = recv5[2 * q + 1, 0:32].astype(F32)
         dvw_ref[:, 128 * q : 128 * q + 128] = jnp.where(
             lane32 < 64, left, pltpu.roll(right, 64, 1)
         )
         parts.append(jnp.where(lane32 < 64, pltpu.roll(left, 64, 1), right).astype(BF16))
     patch_grad = dot(jnp.concatenate(parts, axis=1), vw_v[...], 1, 1)
-    score_grad = recvs[...].reshape(NP, 128).T[0:32].astype(BF16)
+    score_lines = jnp.zeros((16, 128), F32)
+    for chip in range(NP):
+        line = recv5[chip, 32:48].astype(F32)
+        score_lines = jnp.where(row16 == chip, line, score_lines)
+    score_grad = score_lines.T[0:32].astype(BF16)
     dpw_ref[...] = patch_grad + dot(score_grad, kq_v[...])
 
     whole(recv0.at[pl.ds(0, 15)], 0).wait_send()
@@ -395,7 +400,6 @@
     whole(recvr.at[pl.ds(0, 7)], 5).wait_send()
     whole(recvpool.at[pl.ds(0, 15)], 7).wait_send()
     whole(recv5.at[pl.ds(0, 15)], 8).wait_send()
-    whole(recvs.at[pl.ds(0, 15)], 9).wait_send()
     whole(recvq.at[pl.ds(0, 15)], 10).wait_send()
     whole(gtot.at[pl.ds(0, 5)], 12).wait_send()
 
@@ -406,6 +410,15 @@
     @pl.when(jnp.logical_not(has_bias))
     def _():
         whole(quadb, 6).wait_send()
+
+
+def place_kernel(*refs):
+    sources, results, sems = refs[:3], refs[3:6], refs[6]
+    stores = [pltpu.make_async_copy(sources[i], results[i], sems.at[i]) for i in range(3)]
+    for store in stores:
+        store.start()
+    for store in stores:
+        store.wait()
 
 
 def per_device(
@@ -420,18 +433,19 @@
     cotangent,
 ):
     hbm_spec = pl.BlockSpec(memory_space=pltpu.HBM)
-    smem_spec = pl.BlockSpec(memory_space=pltpu.SMEM)
     vmem_spec = pl.BlockSpec(memory_space=pltpu.VMEM)
     aggregated, value_grad, patch_grad = pl.pallas_call(
         pooling_kernel,
         out_shape=(
-            jax.ShapeDtypeStruct((T, D), BF16),
-            jax.ShapeDtypeStruct((32, D), F32),
-            jax.ShapeDtypeStruct((32, D), F32),
+            pltpu.VMEM((T, D), BF16),
+            pltpu.VMEM((32, D), F32),
+            pltpu.VMEM((32, D), F32),
         ),
-        in_specs=[smem_spec] * 2 + [hbm_spec] * 7,
+        in_specs=[hbm_spec] * 9,
         out_specs=(vmem_spec, vmem_spec, vmem_spec),
         scratch_shapes=[
+            pltpu.SMEM((V,), jnp.int32),
+            pltpu.SMEM((2 * NP,), jnp.int32),
             pltpu.VMEM((2, K, 512), BF16),
             pltpu.VMEM((48, D), BF16),
             pltpu.VMEM((16, D), BF16),
@@ -461,11 +475,9 @@
             pltpu.VMEM((NZ, 16, 128), BF16),
             pltpu.VMEM((4, 16, 128), BF16),
             pltpu.VMEM((10, 16, 128), BF16),
-            pltpu.VMEM((NP, T, 128), BF16),
-            pltpu.VMEM((NP, T, 128), BF16),
-            pltpu.VMEM((1, 128), F32),
-            pltpu.VMEM((NP, 1, 128), F32),
-            pltpu.SemaphoreType.DMA((8,)),
+            pltpu.VMEM((NP, 48, 128), BF16),
+            pltpu.VMEM((NP, 48, 128), BF16),
+            pltpu.SemaphoreType.DMA((10,)),
             pltpu.SemaphoreType.DMA((14,)),
             pltpu.SemaphoreType.DMA((14,)),
         ],
@@ -486,6 +498,18 @@
         out_weight,
         cotangent.reshape(T, D),
     )
+    aggregated, value_grad, patch_grad = pl.pallas_call(
+        place_kernel,
+        out_shape=(
+            jax.ShapeDtypeStruct((T, D), BF16),
+            jax.ShapeDtypeStruct((32, D), F32),
+            jax.ShapeDtypeStruct((32, D), F32),
+        ),
+        in_specs=[hbm_spec] * 3,
+        out_specs=(hbm_spec,) * 3,
+        scratch_shapes=[pltpu.SemaphoreType.DMA((3,))],
+        compiler_params=pltpu.CompilerParams(vmem_limit_bytes=4 * 1024 * 1024),
+    )(aggregated, value_grad, patch_grad)
     return (
         aggregated.reshape(1, T, D),
         value_grad,

time: 58.1 us -> 52.1 us (0.90)
  local copies, waits for them, and re-layouts: 4.61 us -> 0 us
  Pallas kernels: 52.7 us -> 51.4 us
    unnamed x3 -> x0, local copies, waits for them, and re-layouts: 4.61 us -> none
    pallas_call x1 -> x2, Pallas kernels: 52.7 us -> 51.4 us  [the longest x1 50.6 us: per_device(): pl.pallas_call(pooling_kernel, out_shape=(pltpu.VMEM((T, D), BF16), pltpu...]
where the time goes in v3:
time: 52.1 us; the launch traced here: 52 us
  Pallas kernels  51.4 us (99%)
  between operations  0.64 us (1%)
    pallas_call x1, Pallas kernels, per_device(): pl.pallas_call(pooling_kernel, out_shape=(pltpu.VMEM((T, D), BF16), pltpu...  50.6 us

profile of v3, /device:TPU:1, one launch (start us, length us, event | category | flops | bytes accessed | tf_op | source)
XLA Modules:
  0.0 52.0 jit_solution(7473042461407636369)
XLA Ops:
  0.6 50.6 %shard_map.112 = (bf16[32,1024]{1,0:T(8,128)(2,1)S(1)}, f32[32,1024]{1,0:T(8,128)S(1)}, f32[32,1024]{1,0:T(8,128)S(1)}) custom-call(s32[16]{0:T(128)} %owner_hbm.1, s32[32]{0:T(128)} %band_hbm.1, bf16[2,16,512]{2,1,0:T(8,128)(2,1)} %fields_hbm.1, bf16[32,1024]{1,0:T(8,128)(2,1)} %bitcast.6, bf16[16,1024]{1,0:T(8,128)(2,1)} %ve_hbm.1, ...), custom_call_target="tpu_custom_call" | custom-call | flops 2000000000 | bytes 5000000 | tf_op jit(solution)/shard_map/pallas_call | solution.py:437
  51.3 0.7 %shard_map.113 = (bf16[32,1024]{1,0:T(8,128)(2,1)}, f32[32,1024]{1,0:T(8,128)}, f32[32,1024]{1,0:T(8,128)}) custom-call(bf16[32,1024]{1,0:T(8,128)(2,1)S(1)} %get-tuple-element.9.refs_0_, f32[32,1024]{1,0:T(8,128)S(1)} %get-tuple-element.10.refs_1_, f32[32,1024]{1,0:T(8,128)S(1)} %get-tuple-element.11.refs_2_), custom_call_target="tpu_custom_call" | custom-call | tf_op jit(solution)/shard_map/pallas_call | solution.py:501

commit v4 on v3

--- a/solution.py
+++ b/solution.py
@@ -362,7 +362,10 @@
     score_line = jnp.broadcast_to(score_parts[0] + score_parts[1], (16, 128)).astype(BF16)
     msg5[:, 0:32, :] = jnp.where(lane32 < 64, value_rows, mine).astype(BF16)
     msg5[:, 32:48, :] = jnp.broadcast_to(score_line, (NP, 16, 128))
-    send_plane(lambda chip: msg5.at[chip], recv5.at[p], 8)
+    for step in PLANE_STEPS:
+        chip = plane_chip(step)
+        slot = {0: 8, 1: 9, 3: 9, 2: 13}[step[0]]
+        send(msg5.at[chip], recv5.at[p], slot, plane_peer(chip))
     recv5[p] = msg5[p]
 
     whole(recvpool.at[pl.ds(0, 15)], 7).wait_recv()
@@ -375,20 +378,28 @@
     agg_ref[...] = (projected * valid).astype(BF16)
 
     loads[7].wait()
-    whole(recv5.at[pl.ds(0, 15)], 8).wait_recv()
-    parts = []
-    for q in range(8):
-        left = recv5[2 * q, 0:32].astype(F32)
-        right = recv5[2 * q + 1, 0:32].astype(F32)
-        dvw_ref[:, 128 * q : 128 * q + 128] = jnp.where(
-            lane32 < 64, left, pltpu.roll(right, 64, 1)
-        )
-        parts.append(jnp.where(lane32 < 64, pltpu.roll(left, 64, 1), right).astype(BF16))
-    patch_grad = dot(jnp.concatenate(parts, axis=1), vw_v[...], 1, 1)
+    patch_grad = jnp.zeros((32, D), F32)
     score_lines = jnp.zeros((16, 128), F32)
-    for chip in range(NP):
-        line = recv5[chip, 32:48].astype(F32)
-        score_lines = jnp.where(row16 == chip, line, score_lines)
+    for i, dx in enumerate((0, 1, 3, 2)):
+        if i == 0:
+            whole(recv5.at[pl.ds(0, 3)], 8).wait_recv()
+        if i == 1:
+            whole(recv5.at[pl.ds(0, 8)], 9).wait_recv()
+        if i == 3:
+            whole(recv5.at[pl.ds(0, 4)], 13).wait_recv()
+        row = lax.rem(x + dx, 4)
+        parts = []
+        for q in range(2):
+            left = recv5[4 * row + 2 * q, 0:32].astype(F32)
+            right = recv5[4 * row + 2 * q + 1, 0:32].astype(F32)
+            at = pl.multiple_of(256 * row + 128 * q, 128)
+            dvw_ref[:, pl.ds(at, 128)] = jnp.where(lane32 < 64, left, pltpu.roll(right, 64, 1))
+            parts.append(jnp.where(lane32 < 64, pltpu.roll(left, 64, 1), right).astype(BF16))
+        columns = vw_v[:, pl.ds(pl.multiple_of(256 * row, 256), 256)]
+        patch_grad = patch_grad + dot(jnp.concatenate(parts, axis=1), columns, 1, 1)
+        for q in range(4):
+            line = recv5[4 * row + q, 32:48].astype(F32)
+            score_lines = jnp.where(row16 == 4 * row + q, line, score_lines)
     score_grad = score_lines.T[0:32].astype(BF16)
     dpw_ref[...] = patch_grad + dot(score_grad, kq_v[...])
 
@@ -399,7 +410,9 @@
     whole(recvp.at[pl.ds(0, 15)], 4).wait_send()
     whole(recvr.at[pl.ds(0, 7)], 5).wait_send()
     whole(recvpool.at[pl.ds(0, 15)], 7).wait_send()
-    whole(recv5.at[pl.ds(0, 15)], 8).wait_send()
+    whole(recv5.at[pl.ds(0, 3)], 8).wait_send()
+    whole(recv5.at[pl.ds(0, 8)], 9).wait_send()
+    whole(recv5.at[pl.ds(0, 4)], 13).wait_send()
     whole(recvq.at[pl.ds(0, 15)], 10).wait_send()
     whole(gtot.at[pl.ds(0, 5)], 12).wait_send()
 

time: 52.1 us -> 51.7 us (level)
  no operation moved by 1% of the time
where the time goes in v4:
time: 51.7 us; the launch traced here: 51.6 us
  Pallas kernels  51 us (99%)
  between operations  0.64 us (1%)
    pallas_call x1, Pallas kernels, per_device(): pl.pallas_call(pooling_kernel, out_shape=(pltpu.VMEM((T, D), BF16), pltpu...  50.2 us

profile of v4, /device:TPU:1, one launch (start us, length us, event | category | flops | bytes accessed | tf_op | source)
XLA Modules:
  0.0 51.6 jit_solution(11333448057672915688)
XLA Ops:
  0.6 50.2 %shard_map.112 = (bf16[32,1024]{1,0:T(8,128)(2,1)S(1)}, f32[32,1024]{1,0:T(8,128)S(1)}, f32[32,1024]{1,0:T(8,128)S(1)}) custom-call(s32[16]{0:T(128)} %owner_hbm.1, s32[32]{0:T(128)} %band_hbm.1, bf16[2,16,512]{2,1,0:T(8,128)(2,1)} %fields_hbm.1, bf16[32,1024]{1,0:T(8,128)(2,1)} %bitcast.6, bf16[16,1024]{1,0:T(8,128)(2,1)} %ve_hbm.1, ...), custom_call_target="tpu_custom_call" | custom-call | flops 2000000000 | bytes 5000000 | tf_op jit(solution)/shard_map/pallas_call | solution.py:450
  50.9 0.7 %shard_map.113 = (bf16[32,1024]{1,0:T(8,128)(2,1)}, f32[32,1024]{1,0:T(8,128)}, f32[32,1024]{1,0:T(8,128)}) custom-call(bf16[32,1024]{1,0:T(8,128)(2,1)S(1)} %get-tuple-element.9.refs_0_, f32[32,1024]{1,0:T(8,128)S(1)} %get-tuple-element.10.refs_1_, f32[32,1024]{1,0:T(8,128)S(1)} %get-tuple-element.11.refs_2_), custom_call_target="tpu_custom_call" | custom-call | tf_op jit(solution)/shard_map/pallas_call | solution.py:514

commit v5 on v4

--- a/solution.py
+++ b/solution.py
@@ -17,6 +17,7 @@
 K = 16
 T = 32
 D = 1024
+DIRECT = 2
 TILES = 9
 FAR_FIRST = (8, 7, 9, 6, 10, 5, 11, 4, 12, 3, 13, 2, 14, 1, 15)
 PLANE_STEPS = sorted(
@@ -73,6 +74,7 @@
     quad,
     quadb,
     recvq,
+    recvx,
     recvqb,
     gtot,
     msg5,
@@ -92,6 +94,9 @@
     def zpeer(d):
         return {"var": lax.rem(z + d, NZ), "lat": lat}
 
+    def other_core(zt):
+        return {"var": zt, "lat": p * 2 + 1 - core}
+
     def plane_chip(step):
         return lax.rem(x + step[0], 4) * 4 + lax.rem(y + step[1], 4)
 
@@ -109,13 +114,20 @@
     own_j = core * 4 + lax.rem(z, 4)
     for d in FAR_FIRST:
         signal(zpeer(d))
+
+    @pl.when(z < DIRECT)
+    def _():
+        for d in FAR_FIRST:
+            signal(other_core(lax.rem(z + d, NZ)))
+
+    @pl.when(z >= DIRECT)
+    def _():
+        for d in range(1, 4):
+            signal(other_core((z // 4) * 4 + lax.rem(z + d, 4)))
+
     for step in PLANE_STEPS:
         signal(plane_peer(plane_chip(step)))
     signal(sibling)
-    for d in range(1, 4):
-        other = (z // 4) * 4 + lax.rem(z + d, 4)
-        signal({"var": other, "lat": p * 2 + 1 - core})
-
     def whole(ref, slot):
         return pltpu.make_async_remote_copy(
             src_ref=ref,
@@ -210,7 +222,7 @@
     packed = jnp.where(lane32 == 97, key_mid, jnp.where(lane32 == 98, key_low, packed))
     wmsg[...] = packed.astype(BF16).reshape(2, 16, 128)
 
-    pl.semaphore_wait(barrier, 34)
+    pl.semaphore_wait(barrier, jnp.where(z < 4, 34, 34 + DIRECT))
 
     for d in FAR_FIRST:
         send(fmsg.at[lax.rem(z + d, NZ)], recv0.at[z], 0, zpeer(d))
@@ -299,6 +311,8 @@
 
     whole(recvr.at[pl.ds(0, 7)], 5).wait_recv()
     quad[...] = jnp.sum(recvr[...].astype(F32), axis=0).astype(BF16)
+    for zt in range(DIRECT):
+        send(quad, recvx.at[z], 14, other_core(zt))
     for d in FAR_FIRST:
         send(quad, recvq.at[z], 10, zpeer(d))
     recvq[z] = quad[...]
@@ -307,6 +321,8 @@
     def _():
         whole(recvb.at[pl.ds(0, 7)], 6).wait_recv()
         quadb[...] = jnp.sum(recvb[...].astype(F32), axis=0).astype(BF16)
+        for zt in range(DIRECT):
+            send(quadb, recvqb.at[z // 4], 11, other_core(zt))
         for d in FAR_FIRST:
             send(quadb, recvqb.at[z // 4], 11, zpeer(d))
         recvqb[z // 4] = quadb[...]
@@ -316,28 +332,40 @@
 
     whole(recvp.at[pl.ds(0, 15)], 4).wait_recv()
     whole(recvq.at[pl.ds(0, 15)], 10).wait_recv()
-    half = jnp.sum(recvq[...].astype(F32).reshape(4, 4, 16, 128), axis=0).astype(BF16)
     half_at = pl.multiple_of(5 * core, 5)
-    gtot[pl.ds(half_at, 4)] = half
-
-    @pl.when(core == 1)
+    rest_at = pl.multiple_of(5 - 5 * core, 5)
+    direct = z < DIRECT
+
+    def four_tiles(ref):
+        return jnp.sum(ref[...].astype(F32).reshape(4, 4, 16, 128), axis=0).astype(BF16)
+
+    gtot[pl.ds(half_at, 4)] = four_tiles(recvq)
+
+    @pl.when((core == 0) & has_bias)
+    def _():
+        whole(recvqb.at[pl.ds(0, 3)], 11).wait_recv()
+
+    @pl.when(((core == 0) & jnp.logical_not(has_bias)) | ((core == 1) & direct))
+    def _():
+        whole(recvqb, 11).wait_recv()
+
+    @pl.when((core == 0) | direct)
+    def _():
+        gtot[4] = jnp.sum(recvqb[...].astype(F32), axis=0).astype(BF16)
+
+    @pl.when((core == 1) & jnp.logical_not(direct))
     def _():
         gtot[9] = jnp.zeros((16, 128), BF16)
 
-    @pl.when((core == 0) & has_bias)
-    def _():
-        whole(recvqb.at[pl.ds(0, 3)], 11).wait_recv()
-
-    @pl.when((core == 0) & jnp.logical_not(has_bias))
-    def _():
-        whole(recvqb, 11).wait_recv()
-
-    @pl.when(core == 0)
-    def _():
-        gtot[4] = jnp.sum(recvqb[...].astype(F32), axis=0).astype(BF16)
-
-    send(gtot.at[pl.ds(half_at, 5)], gtot.at[pl.ds(half_at, 5)], 12, sibling)
-    whole(gtot.at[pl.ds(0, 5)], 12).wait_recv()
+    @pl.when(direct)
+    def _():
+        whole(recvx, 14).wait_recv()
+        gtot[pl.ds(rest_at, 4)] = four_tiles(recvx)
+
+    @pl.when(jnp.logical_not(direct))
+    def _():
+        send(gtot.at[pl.ds(half_at, 5)], gtot.at[pl.ds(half_at, 5)], 12, sibling)
+        whole(gtot.at[pl.ds(0, 5)], 12).wait_recv()
 
     bias_rows = pwve[pl.ds(32, 16)]
     rows_all = recvp[...].reshape(TOK, VK)
@@ -414,11 +442,16 @@
     whole(recv5.at[pl.ds(0, 8)], 9).wait_send()
     whole(recv5.at[pl.ds(0, 4)], 13).wait_send()
     whole(recvq.at[pl.ds(0, 15)], 10).wait_send()
-    whole(gtot.at[pl.ds(0, 5)], 12).wait_send()
+    whole(recvx.at[pl.ds(0, DIRECT)], 14).wait_send()
+
+    @pl.when(jnp.logical_not(direct))
+    def _():
+        whole(gtot.at[pl.ds(0, 5)], 12).wait_send()
+
 
     @pl.when(has_bias)
     def _():
-        whole(recvq.at[pl.ds(0, 15)], 11).wait_send()
+        whole(recv1.at[pl.ds(0, 15 + DIRECT)], 11).wait_send()
 
     @pl.when(jnp.logical_not(has_bias))
     def _():
@@ -486,13 +519,14 @@
             pltpu.VMEM((16, 128), BF16),
             pltpu.VMEM((16, 128), BF16),
             pltpu.VMEM((NZ, 16, 128), BF16),
+            pltpu.VMEM((NZ, 16, 128), BF16),
             pltpu.VMEM((4, 16, 128), BF16),
             pltpu.VMEM((10, 16, 128), BF16),
             pltpu.VMEM((NP, 48, 128), BF16),
             pltpu.VMEM((NP, 48, 128), BF16),
             pltpu.SemaphoreType.DMA((10,)),
-            pltpu.SemaphoreType.DMA((14,)),
-            pltpu.SemaphoreType.DMA((14,)),
+            pltpu.SemaphoreType.DMA((15,)),
+            pltpu.SemaphoreType.DMA((15,)),
         ],
         compiler_params=pltpu.CompilerParams(
             collective_id=0, has_side_effects=True, vmem_limit_bytes=60 * 1024 * 1024

time: 51.7 us -> 50.2 us (0.971)
  Pallas kernels: 51 us -> 49.4 us
    pallas_call x1, Pallas kernels: 50.2 us -> 48.7 us  [per_device(): pl.pallas_call(pooling_kernel, out_shape=(pltpu.VMEM((T, D), BF16), pltpu...]
where the time goes in v5:
time: 50.2 us; the launch traced here: 50.1 us
  Pallas kernels  49.4 us (98%)
  between operations  0.64 us (1%)
    pallas_call x1, Pallas kernels, per_device(): pl.pallas_call(pooling_kernel, out_shape=(pltpu.VMEM((T, D), BF16), pltpu...  48.7 us

profile of v5, /device:TPU:1, one launch (start us, length us, event | category | flops | bytes accessed | tf_op | source)
XLA Modules:
  0.0 50.1 jit_solution(7143556461317424955)
XLA Ops:
  0.6 48.7 %shard_map.112 = (bf16[32,1024]{1,0:T(8,128)(2,1)S(1)}, f32[32,1024]{1,0:T(8,128)S(1)}, f32[32,1024]{1,0:T(8,128)S(1)}) custom-call(s32[16]{0:T(128)} %owner_hbm.1, s32[32]{0:T(128)} %band_hbm.1, bf16[2,16,512]{2,1,0:T(8,128)(2,1)} %fields_hbm.1, bf16[32,1024]{1,0:T(8,128)(2,1)} %bitcast.6, bf16[16,1024]{1,0:T(8,128)(2,1)} %ve_hbm.1, ...), custom_call_target="tpu_custom_call" | custom-call | flops 2000000000 | bytes 5000000 | tf_op jit(solution)/shard_map/pallas_call | solution.py:483
  49.3 0.7 %shard_map.113 = (bf16[32,1024]{1,0:T(8,128)(2,1)}, f32[32,1024]{1,0:T(8,128)}, f32[32,1024]{1,0:T(8,128)}) custom-call(bf16[32,1024]{1,0:T(8,128)(2,1)S(1)} %get-tuple-element.9.refs_0_, f32[32,1024]{1,0:T(8,128)S(1)} %get-tuple-element.10.refs_1_, f32[32,1024]{1,0:T(8,128)S(1)} %get-tuple-element.11.refs_2_), custom_call_target="tpu_custom_call" | custom-call | tf_op jit(solution)/shard_map/pallas_call | solution.py:548

commit v6 on v5

--- a/solution.py
+++ b/solution.py
@@ -241,8 +241,9 @@
     head_grads = dot(masked, ow_v[...], 1, 1)
     for q in range(8):
         two = head_grads[:, 128 * q : 128 * q + 128]
-        hmsg[2 * q] = jnp.where(lane32 < 64, two, 0.0).astype(BF16)
-        hmsg[2 * q + 1] = jnp.where(lane32 < 64, pltpu.roll(two, 64, 1), 0.0).astype(BF16)
+        turned = pltpu.roll(two, 64, 1)
+        hmsg[2 * q] = jnp.where(lane16 < 64, two[0:16], turned[16:32]).astype(BF16)
+        hmsg[2 * q + 1] = jnp.where(lane16 < 64, turned[0:16], two[16:32]).astype(BF16)
 
     send_plane(lambda chip: hmsg.at[chip], recvh.at[p], 2)
     recvh[p] = hmsg[p]
@@ -268,6 +269,10 @@
     send_plane(lambda chip: pturn, recvp.at[p], 4)
     recvp[p] = pturn[...]
 
+    whole(recvh.at[pl.ds(0, 15)], 2).wait_recv()
+    packed = recvh[...].astype(F32)
+    unpacked = jnp.concatenate([packed, pltpu.roll(packed, 64, 2)], axis=1)
+    grads = jnp.where(lane32 < 64, unpacked, 0.0).astype(BF16).reshape(TOK, 128)
     whole(recvf.at[pl.ds(0, 15)], 3).wait_recv()
     pixels = recvf[...].reshape(TOK, VK).astype(F32).T.reshape(V, K, TOK)
     scores = jnp.sum(pixels * key_rows, axis=1) + key_bias
@@ -276,8 +281,6 @@
     weighted = pixels * attention[:, None, :]
     aa[pl.ds(0, VK)] = weighted.reshape(VK, TOK).astype(BF16)
     aa[pl.ds(VK, V)] = attention.astype(BF16)
-    whole(recvh.at[pl.ds(0, 15)], 2).wait_recv()
-    grads = recvh[...].reshape(TOK, 128)
     head_weights = mm[...].reshape(VK + V, 128)
     lhs = aa[...]
     sums = dot(lhs, grads)
@@ -331,6 +334,15 @@
     recvpool[p] = pmsg[p]
 
     whole(recvp.at[pl.ds(0, 15)], 4).wait_recv()
+    whole(recvpool.at[pl.ds(0, 15)], 7).wait_recv()
+    parts = []
+    for q in range(8):
+        left = recvpool[2 * q].astype(F32)
+        right = recvpool[2 * q + 1].astype(F32)
+        parts.append(jnp.where(lane32 < 64, left, pltpu.roll(right, 64, 1)).astype(BF16))
+    projected = dot(jnp.concatenate(parts, axis=1), ow_v[...])
+    agg_ref[...] = (projected * valid).astype(BF16)
+
     whole(recvq.at[pl.ds(0, 15)], 10).wait_recv()
     half_at = pl.multiple_of(5 * core, 5)
     rest_at = pl.multiple_of(5 - 5 * core, 5)
@@ -395,15 +407,6 @@
         slot = {0: 8, 1: 9, 3: 9, 2: 13}[step[0]]
         send(msg5.at[chip], recv5.at[p], slot, plane_peer(chip))
     recv5[p] = msg5[p]
-
-    whole(recvpool.at[pl.ds(0, 15)], 7).wait_recv()
-    parts = []
-    for q in range(8):
-        left = recvpool[2 * q].astype(F32)
-        right = recvpool[2 * q + 1].astype(F32)
-        parts.append(jnp.where(lane32 < 64, left, pltpu.roll(right, 64, 1)).astype(BF16))
-    projected = dot(jnp.concatenate(parts, axis=1), ow_v[...])
-    agg_ref[...] = (projected * valid).astype(BF16)
 
     loads[7].wait()
     patch_grad = jnp.zeros((32, D), F32)
@@ -503,8 +506,8 @@
             pltpu.VMEM((NZ, K, 128), BF16),
             pltpu.VMEM((2, K, 128), BF16),
             pltpu.VMEM((2 * NZ, K, 128), BF16),
-            pltpu.VMEM((NP, T, 128), BF16),
-            pltpu.VMEM((NP, T, 128), BF16),
+            pltpu.VMEM((NP, 16, 128), BF16),
+            pltpu.VMEM((NP, 16, 128), BF16),
             pltpu.VMEM((V + 1, K, 128), BF16),
             pltpu.VMEM((T, VK), BF16),
             pltpu.VMEM((32, VK), BF16),

time: 50.2 us -> 50.1 us (level)
  no operation moved by 1% of the time
where the time goes in v6:
time: 50.1 us; the launch traced here: 49.9 us
  Pallas kernels  49.3 us (98%)
  between operations  0.64 us (1%)
    pallas_call x1, Pallas kernels, per_device(): pl.pallas_call(pooling_kernel, out_shape=(pltpu.VMEM((T, D), BF16), pltpu...  48.5 us

profile of v6, /device:TPU:1, one launch (start us, length us, event | category | flops | bytes accessed | tf_op | source)
XLA Modules:
  0.0 49.9 jit_solution(1472030338722901753)
XLA Ops:
  0.6 48.5 %shard_map.112 = (bf16[32,1024]{1,0:T(8,128)(2,1)S(1)}, f32[32,1024]{1,0:T(8,128)S(1)}, f32[32,1024]{1,0:T(8,128)S(1)}) custom-call(s32[16]{0:T(128)} %owner_hbm.1, s32[32]{0:T(128)} %band_hbm.1, bf16[2,16,512]{2,1,0:T(8,128)(2,1)} %fields_hbm.1, bf16[32,1024]{1,0:T(8,128)(2,1)} %bitcast.6, bf16[16,1024]{1,0:T(8,128)(2,1)} %ve_hbm.1, ...), custom_call_target="tpu_custom_call" | custom-call | flops 2000000000 | bytes 5000000 | tf_op jit(solution)/shard_map/pallas_call | solution.py:486
  49.2 0.7 %shard_map.113 = (bf16[32,1024]{1,0:T(8,128)(2,1)}, f32[32,1024]{1,0:T(8,128)}, f32[32,1024]{1,0:T(8,128)}) custom-call(bf16[32,1024]{1,0:T(8,128)(2,1)S(1)} %get-tuple-element.9.refs_0_, f32[32,1024]{1,0:T(8,128)S(1)} %get-tuple-element.10.refs_1_, f32[32,1024]{1,0:T(8,128)S(1)} %get-tuple-element.11.refs_2_), custom_call_target="tpu_custom_call" | custom-call | tf_op jit(solution)/shard_map/pallas_call | solution.py:551

commit v7 on v6

--- a/solution.py
+++ b/solution.py
@@ -309,8 +309,9 @@
     def _():
         send(gtile.at[8], recvb.at[own_j], 6, quad_device(jnp.int32(1)))
 
-    pooled = dot(lhs, head_weights, 0, 0)
-    pmsg[...] = pooled.astype(BF16).reshape(NP, T, 128)
+    pooled = dot(lhs, head_weights, 0, 0).reshape(NP, T, 128)
+    beside = pltpu.roll(pooled[:, 16:32], 64, 2)
+    pmsg[...] = jnp.where(lane16 < 64, pooled[:, 0:16], beside).astype(BF16)
 
     whole(recvr.at[pl.ds(0, 7)], 5).wait_recv()
     quad[...] = jnp.sum(recvr[...].astype(F32), axis=0).astype(BF16)
@@ -339,7 +340,9 @@
     for q in range(8):
         left = recvpool[2 * q].astype(F32)
         right = recvpool[2 * q + 1].astype(F32)
-        parts.append(jnp.where(lane32 < 64, left, pltpu.roll(right, 64, 1)).astype(BF16))
+        upper = jnp.where(lane16 < 64, left, pltpu.roll(right, 64, 1))
+        lower = jnp.where(lane16 < 64, pltpu.roll(left, 64, 1), right)
+        parts.append(jnp.concatenate([upper, lower], axis=0).astype(BF16))
     projected = dot(jnp.concatenate(parts, axis=1), ow_v[...])
     agg_ref[...] = (projected * valid).astype(BF16)
 
@@ -514,8 +517,8 @@
             pltpu.VMEM((NP, T, VK), BF16),
             pltpu.VMEM((NP, T, VK), BF16),
             pltpu.VMEM((VK + V, TOK), BF16),
-            pltpu.VMEM((NP, T, 128), BF16),
-            pltpu.VMEM((NP, T, 128), BF16),
+            pltpu.VMEM((NP, 16, 128), BF16),
+            pltpu.VMEM((NP, 16, 128), BF16),
             pltpu.VMEM((TILES, 16, 128), BF16),
             pltpu.VMEM((8, 16, 128), BF16),
             pltpu.VMEM((8, 16, 128), BF16),

time: 50.1 us -> 50.1 us (level)
  no operation moved by 1% of the time
where the time goes in v7:
time: 50.1 us; the launch traced here: 49.9 us
  Pallas kernels  49.3 us (98%)
  between operations  0.64 us (1%)
    pallas_call x1, Pallas kernels, per_device(): pl.pallas_call(pooling_kernel, out_shape=(pltpu.VMEM((T, D), BF16), pltpu...  48.5 us

profile of v7, /device:TPU:1, one launch (start us, length us, event | category | flops | bytes accessed | tf_op | source)
XLA Modules:
  0.0 49.9 jit_solution(4564351735134809143)
XLA Ops:
  0.6 48.5 %shard_map.112 = (bf16[32,1024]{1,0:T(8,128)(2,1)S(1)}, f32[32,1024]{1,0:T(8,128)S(1)}, f32[32,1024]{1,0:T(8,128)S(1)}) custom-call(s32[16]{0:T(128)} %owner_hbm.1, s32[32]{0:T(128)} %band_hbm.1, bf16[2,16,512]{2,1,0:T(8,128)(2,1)} %fields_hbm.1, bf16[32,1024]{1,0:T(8,128)(2,1)} %bitcast.6, bf16[16,1024]{1,0:T(8,128)(2,1)} %ve_hbm.1, ...), custom_call_target="tpu_custom_call" | custom-call | flops 2000000000 | bytes 5000000 | tf_op jit(solution)/shard_map/pallas_call | solution.py:489
  49.2 0.7 %shard_map.113 = (bf16[32,1024]{1,0:T(8,128)(2,1)}, f32[32,1024]{1,0:T(8,128)}, f32[32,1024]{1,0:T(8,128)}) custom-call(bf16[32,1024]{1,0:T(8,128)(2,1)S(1)} %get-tuple-element.9.refs_0_, f32[32,1024]{1,0:T(8,128)S(1)} %get-tuple-element.10.refs_1_, f32[32,1024]{1,0:T(8,128)S(1)} %get-tuple-element.11.refs_2_), custom_call_target="tpu_custom_call" | custom-call | tf_op jit(solution)/shard_map/pallas_call | solution.py:554
